TPU v7x, 256 devices: a whole 4x4x8 slice. The times are simulated.
256 devices in a mesh: tm: 64 (over z, y_hi, x), patch: 4 (over y_lo, core).
Axes of the slice: x: 4, y: 4 (y_hi: 2, y_lo: 2; y = y_hi * 2 + y_lo), z: 8, core: 2. Of those that a mesh axis runs over, the one named last changes fastest.
Arguments:
- tokens: float32 [1, 128, 256, 768], P(None, 'tm', 'patch'), may hold values from -6 to 6
- norm_gain_vector: float32 [768], replicated, may hold values from 0.1 to 1.9
- qkv_weight: float32 [768, 2304], replicated, may hold values from -4 to 4
- out_weight: float32 [768, 768], replicated, may hold values from -0.21875 to 0.21875
- upstream: float32 [1, 128, 256, 768], P(None, 'tm', 'patch'), may hold values from -6 to 6
Outputs:
- output: float32 [1, 128, 256, 768], P(None, 'tm', 'patch')
- tokens_grad: float32 [1, 128, 256, 768], P(None, 'tm', 'patch')
- qkv_grad: float32 [768, 2304], P('tm')
- out_grad: float32 [768, 768], P('tm')
- gain_grad: float32 [768], P('tm')
All inputs are finite; a program needn't handle non-finite values.
Results may differ from a plain program's by a relative error of at most 0.0003.
Values sent between devices are 32-bit elements; how exact they have to be, the bound alone decides.
A program may use at most 128 MiB of HBM per device.

v0:
```python
import jax
import jax.numpy as jnp
from jax import lax
from jax.sharding import PartitionSpec as P

HEADS = 12
HEAD_DIM = 64


HIGH = lax.Precision.HIGHEST


def project(left, weight):
    return jnp.einsum("bfpd,de->bfpe", left, weight, precision=HIGH)


def weight_terms(left, right):
    return jnp.einsum("bfpd,bfpe->de", left, right, precision=HIGH)


def apply_layer_norm(tokens, norm_gain_vector):
    input_average = jnp.mean(tokens, axis=-1, keepdims=True)
    centered_input = tokens - input_average
    var = jnp.mean(centered_input * centered_input, axis=-1, keepdims=True)
    inverse_deviation = lax.rsqrt(var + 1e-05)
    standardized_input = centered_input * inverse_deviation
    return (standardized_input * norm_gain_vector, standardized_input, inverse_deviation)


def norm_backward(
    normalized_input_gradient, standardized_input, inverse_deviation, norm_gain_vector
):
    normalized_gradient = normalized_input_gradient * norm_gain_vector
    first_result = jnp.mean(normalized_gradient, axis=-1, keepdims=True)
    second_result = jnp.mean(normalized_gradient * standardized_input, axis=-1, keepdims=True)
    gain_products = jnp.sum(normalized_input_gradient * standardized_input, axis=(0, 1, 2))
    return (
        inverse_deviation
        * (normalized_gradient - first_result - standardized_input * second_result),
        gain_products,
    )


def split_heads(qkv, heads, head_dim):
    shaped = qkv.reshape(qkv.shape[:3] + (3, heads, head_dim))
    return (shaped[:, :, :, 0], shaped[:, :, :, 1], shaped[:, :, :, 2])


def attend(qkv, heads, head_dim):
    query, keys, values = split_heads(qkv, heads, head_dim)
    scores = jnp.einsum("bfphe,bgphe->bphfg", query, keys, precision=HIGH) / jnp.sqrt(
        jnp.float32(head_dim)
    )
    probs = jax.nn.softmax(scores, axis=-1)
    mix = jnp.einsum("bphfg,bgphe->bfphe", probs, values, precision=HIGH)
    return (mix.reshape(qkv.shape[:3] + (heads * head_dim,)), probs)


def attend_back(mix_grad, qkv, probs, heads, head_dim):
    query, keys, values = split_heads(qkv, heads, head_dim)
    heads_grad = mix_grad.reshape(mix_grad.shape[:3] + (heads, head_dim))
    values_grad = jnp.einsum("bphfg,bfphe->bgphe", probs, heads_grad, precision=HIGH)
    probs_grad = jnp.einsum("bfphe,bgphe->bphfg", heads_grad, values, precision=HIGH)
    scores_grad = probs * (probs_grad - jnp.sum(probs_grad * probs, axis=-1, keepdims=True))
    scores_grad = scores_grad / jnp.sqrt(jnp.float32(head_dim))
    query_grad = jnp.einsum("bphfg,bgphe->bfphe", scores_grad, keys, precision=HIGH)
    keys_grad = jnp.einsum("bphfg,bfphe->bgphe", scores_grad, query, precision=HIGH)
    stacked = jnp.stack([query_grad, keys_grad, values_grad], axis=3)
    return stacked.reshape(qkv.shape)


def run_layer(
    tokens,
    upstream,
    norm_gain_vector,
    qkv_weight,
    out_weight,
    to_patch_wide,
    to_frame_narrow,
    to_patch_narrow,
    to_frame_wide,
):
    heads = HEADS
    head_dim = HEAD_DIM
    normalized_input, standardized_input, inverse_deviation = apply_layer_norm(
        tokens, norm_gain_vector
    )
    qkv = project(normalized_input, qkv_weight)
    qkv_local = to_patch_wide(qkv)
    mix_local, probs = attend(qkv_local, heads, head_dim)
    mix = to_frame_narrow(mix_local)
    output = tokens + project(mix, out_weight)
    out_terms = weight_terms(mix, upstream)
    mix_grad = to_patch_narrow(project(upstream, out_weight.T))
    qkv_grad_local = attend_back(mix_grad, qkv_local, probs, heads, head_dim)
    qkv_grad = to_frame_wide(qkv_grad_local)
    qkv_terms = weight_terms(normalized_input, qkv_grad)
    normalized_input_gradient = project(qkv_grad, qkv_weight.T)
    backward_pass, gain_products = norm_backward(
        normalized_input_gradient, standardized_input, inverse_deviation, norm_gain_vector
    )
    return (output, upstream + backward_pass, qkv_terms, out_terms, gain_products)


def body(tokens, norm_gain_vector, qkv_weight, out_weight, upstream):
    output, tokens_grad, qkv_terms, out_terms, gain_products = run_layer(
        tokens,
        upstream,
        norm_gain_vector,
        qkv_weight,
        out_weight,
        lambda value: lax.all_to_all(value, "tm", split_axis=2, concat_axis=1, tiled=True),
        lambda value: lax.all_to_all(value, "tm", split_axis=1, concat_axis=2, tiled=True),
        lambda value: lax.all_to_all(value, "tm", split_axis=2, concat_axis=1, tiled=True),
        lambda value: lax.all_to_all(value, "tm", split_axis=1, concat_axis=2, tiled=True),
    )
    qkv_rows, out_rows, gain_rows = (
        lax.psum_scatter(qkv_terms, "tm", scatter_dimension=0, tiled=True),
        lax.psum_scatter(out_terms, "tm", scatter_dimension=0, tiled=True),
        lax.psum_scatter(gain_products, "tm", scatter_dimension=0, tiled=True),
    )
    qkv_grad, out_grad, gain_grad = lax.psum((qkv_rows, out_rows, gain_rows), "patch")
    return (output, tokens_grad, qkv_grad, out_grad, gain_grad)


def solution(mesh):
    in_specs = (P(None, "tm", "patch", None), P(), P(), P(), P(None, "tm", "patch", None))
    out_specs = (
        P(None, "tm", "patch", None),
        P(None, "tm", "patch", None),
        P("tm", None),
        P("tm", None),
        P("tm"),
    )
    return jax.shard_map(body, mesh=mesh, in_specs=in_specs, out_specs=out_specs, check_vma=False)
```

profile of v0, /device:TPU:1, one launch (start us, length us, event | category | flops | bytes accessed | tf_op | source)
XLA Modules:
  0.0 791.6 jit_solution(15910527254553311083)
XLA Ops:
  8.8 3.5 fusion.16
  13.4 15.1 %all-to-all-start.2 = ((f32[1,2,64,768]{3,1,0,2:T(2,128)}), f32[1,2,64,768]{3,1,0,2:T(2,128)S(1)}, u32[]{:S(2)}, u32[]{:S(2)}) async-start(f32[1,2,64,768]{3,1,0,2:T(2,128)} %copy.36), calls=%async_computation.2 | async-start | bytes 786432 | tf_op jit(solution)/shard_map/all_to_all | solution.py:114
  28.9 6.4 fusion.6
  35.2 2.0 copy.29
  37.2 5.0 all-to-all-done.2
  42.2 8.6 %all-to-all-start = ((f32[1,2,64,2304]{3,1,0,2:T(2,128)}), f32[1,2,64,2304]{3,1,0,2:T(2,128)}, u32[]{:S(2)}, u32[]{:S(2)}) async-start(f32[1,2,64,2304]{3,1,0,2:T(2,128)} %copy.29), calls=%async_computation | async-start | bytes 2359296 | tf_op jit(solution)/shard_map/all_to_all | solution.py:112
  52.3 2.3 copy.37
  54.6 24.5 %all-to-all-done = f32[1,2,64,2304]{3,1,0,2:T(2,128)} async-done(((f32[1,2,64,2304]{3,1,0,2:T(2,128)}), f32[1,2,64,2304]{3,1,0,2:T(2,128)}, u32[]{:S(2)}, u32[]{:S(2)}) %all-to-all-start) | async-done | bytes 1179680 | tf_op jit(solution)/shard_map/all_to_all | solution.py:112
  79.1 3.6 reshape.154
  82.7 3.6 fusion.63
  86.3 2.3 copy.48
  97.5 9.3 %all-to-all-start.1 = ((f32[1,128,1,768]{3,2,0,1:T(1,128)}), f32[1,128,1,768]{3,2,0,1:T(1,128)S(1)}, u32[]{:S(2)}, u32[]{:S(2)}) async-start(f32[1,128,1,768]{3,2,0,1:T(1,128)} %copy.34), calls=%async_computation.1 | async-start | bytes 786432 | tf_op jit(solution)/shard_map/all_to_all | solution.py:113
  106.9 2.9 multiply_reduce_fusion
  115.2 3.8 copy.42
  119.4 11.9 %all-to-all-start.3 = ((f32[1,128,1,2304]{3,2,0,1:T(1,128)}), f32[1,128,1,2304]{3,2,0,1:T(1,128)}, u32[]{:S(2)}, u32[]{:S(2)}) async-start(f32[1,128,1,2304]{3,2,0,1:T(1,128)} %copy.42), calls=%async_computation.3 | async-start | bytes 2359296 | tf_op jit(solution)/shard_map/all_to_all | solution.py:115
  131.4 3.5 convolution_bitcast_fusion.1
  134.9 23.2 %all-to-all-done.3 = f32[1,128,1,2304]{3,2,0,1:T(1,128)} async-done(((f32[1,128,1,2304]{3,2,0,1:T(1,128)}), f32[1,128,1,2304]{3,2,0,1:T(1,128)}, u32[]{:S(2)}, u32[]{:S(2)}) %all-to-all-start.3) | async-done | bytes 1179680 | tf_op jit(solution)/shard_map/all_to_all | solution.py:115
  158.2 9.2 %convolution_bitcast_fusion = f32[768,2304]{1,0:T(8,128)} fusion(f32[1,64,2,1,2304]{4,3,2,1,0:T(1,128)} %bitcast.30, f32[1,2,64,768]{3,2,1,0:T(8,128)S(1)} %copy-done.1, f32[768]{0:T(1024)S(1)} %copy-done.10, f32[2,64]{1,0:T(2,128)S(1)} %add_rsqrt_fusion, f32[2,64]{1,0:T(2,128)S(1)} %broadcast_multiply_fusion.2), kind=kOutput, calls=%fused_computation.4 | convolution fusion | flops 2718203904 | bytes 8654848 | tf_op jit(solution)/shard_map/bfpd,bfpe->de/dot_general | solution.py:18
  167.3 189.7 %fusion.62 = (f32[16,2304]{1,0:T(8,128)}, f32[16,768]{1,0:T(8,128)}) fusion(f32[768,2304]{1,0:T(8,128)} %convolution_bitcast_fusion, f32[768,768]{1,0:T(8,128)} %convolution_bitcast_fusion.1), kind=kCustom, calls=%all-reduce-scatter.2 | all-reduce-scatter fusion | flops 3145729 | bytes 9634816
  359.7 9.0 %collective-permute-start.31 = (f32[12,768]{1,0:T(8,128)S(1)}, f32[12,768]{1,0:T(8,128)}, u32[]{:S(2)}, u32[]{:S(2)}) collective-permute-start(f32[12,768]{1,0:T(8,128)S(1)} %slice.19), channel_id=1, source_target_pairs={{0,64},{4,68},{8,72},{12,76},{16,80},{20,84},{24,88},{28,92},{32,9... | collective-permute-start | bytes 110600
  376.2 6.0 collective-permute-start.25
  384.2 4.6 collective-permute-start.24
  390.1 3.4 collective-permute-start.22
  393.6 3.2 collective-permute-start.21
  396.8 4.3 collective-permute-start.20
  401.1 2.2 fusion.19
  405.8 3.6 collective-permute-start.18
  409.5 4.9 collective-permute-start.17
  416.4 2.1 collective-permute-start.15
  418.5 10.7 %fusion.28 = (f32[768]{0:T(1024)S(1)}, f32[2,64]{1,0:T(2,128)S(1)}, f32[2,64,768]{2,1,0:T(8,128)S(1)}) fusion(f32[1,2,64,768]{3,2,1,0:T(8,128)S(1)} %copy-done.1, f32[2,64]{1,0:T(2,128)S(1)} %add_rsqrt_fusion, f32[2,64]{1,0:T(2,128)S(1)} %broadcast_multiply_fusion.2, f32[768]{0:T(1024)S(1)} %copy-done.10, f32[768,2304]{1,0:T(8,128)} %param.7, ...), kind=kOutput, calls=%fused_computation.29 | convolution fusion | flops 2718596096 | bytes 9051648 | tf_op jit(solution)/shard_map/bfpd,de->bfpe/dot_general | solution.py:14
  429.3 4.4 collective-permute-start.14
  435.6 1.9 collective-permute-start.12
  437.6 1.9 collective-permute-start.11
  439.5 2.2 collective-permute-start.10
  442.4 151.1 %all-reduce.2 = f32[768]{0:T(1024)} all-reduce(f32[768]{0:T(1024)S(1)} %get-tuple-element.5), channel_id=4, replica_groups=mesh['tm'=64,'patch'=4] {'tm'}, use_global_device_ids=true, to_apply=%region_12.0.clone | all-reduce | flops 768 | bytes 6144
  594.4 1.9 collective-permute-start.9
  596.3 1.9 collective-permute-start.8
  598.3 2.0 collective-permute-start.7
  600.2 4.0 collective-permute-start.6
  604.2 7.9 collective-permute-start.5
  612.1 2.0 collective-permute-start.4
  614.1 4.0 collective-permute-start.3
  618.1 2.3 collective-permute-start.2
  620.4 4.9 collective-permute-start.1
  628.8 25.0 %concatenate.1 = f32[268,768]{1,0:T(8,128)} concatenate(f32[12,768]{1,0:T(8,128)} %collective-permute-done.31, f32[16,768]{1,0:T(8,128)} %collective-permute-done.30, f32[16,768]{1,0:T(8,128)} %collective-permute-done.29, f32[16,768]{1,0:T(8,128)} %collective-permute-done.28, f32[16,768]{1,0:T(8,128)} %collective-permute-done.27, f32[16,768]{1,0:T(8,128)} %collective-permute-done.26, ...), dimensions={0} | concatenate | bytes 1646592
  653.8 29.0 %concatenate = f32[268,2304]{1,0:T(8,128)} concatenate(f32[12,2304]{1,0:T(8,128)} %collective-permute-done.15, f32[16,2304]{1,0:T(8,128)} %collective-permute-done.14, f32[16,2304]{1,0:T(8,128)} %collective-permute-done.13, f32[16,2304]{1,0:T(8,128)} %collective-permute-done.12, f32[16,2304]{1,0:T(8,128)} %collective-permute-done.11, f32[16,2304]{1,0:T(8,128)} %collective-permute-done.10, ...), dimensions={0} | concatenate | bytes 4939776
  685.4 63.6 %all-reduce.5 = (f32[12,768]{1,0:T(8,128)}, f32[12]{0:T(128)}) all-reduce(f32[12,768]{1,0:T(8,128)S(1)} %constant_dynamic-slice_fusion, f32[12]{0:T(128)S(1)} %dynamic-slice.5), channel_id=1, replica_groups=mesh['tm'=64,'patch'=4] {'patch'}, use_global_device_ids=true, to_apply=%region_10.0 | all-reduce | flops 9228 | bytes 73824 | tf_op jit(solution)/shard_map/psum | solution.py:122
  749.0 33.9 %all-reduce.9.cloned.1.call-done = f32[12,2304]{1,0:T(8,128)} async-done(((f32[12,2304]{1,0:T(8,128)}), f32[12,2304]{1,0:T(8,128)}) %all-reduce.9.cloned.1.call-update) | async-done | bytes 110608 | tf_op jit(solution)/shard_map/psum | solution.py:122
  (122 shorter events, 47.0 us)
Async XLA Ops:
  7.2 21.4 %copy-start.1 = (f32[1,2,64,768]{3,2,1,0:T(8,128)S(1)}, f32[1,2,64,768]{3,2,1,0:T(8,128)}, u32[]{:S(2)}) copy-start(f32[1,2,64,768]{3,2,1,0:T(8,128)} %param.5) | copy-start | bytes 1179652
  8.8 20.0 %copy-start.10 = (f32[768]{0:T(1024)S(1)}, f32[768]{0:T(1024)}, u32[]{:S(2)}) copy-start(f32[768]{0:T(1024)} %param.6) | copy-start | bytes 9220
  13.4 28.8 %all-to-all-start.2 = ((f32[1,2,64,768]{3,1,0,2:T(2,128)}), f32[1,2,64,768]{3,1,0,2:T(2,128)S(1)}, u32[]{:S(2)}, u32[]{:S(2)}) async-start(f32[1,2,64,768]{3,1,0,2:T(2,128)} %copy.36), calls=%async_computation.2 | async-start | bytes 786432 | tf_op jit(solution)/shard_map/all_to_all | solution.py:114
  42.2 36.9 %all-to-all-start = ((f32[1,2,64,2304]{3,1,0,2:T(2,128)}), f32[1,2,64,2304]{3,1,0,2:T(2,128)}, u32[]{:S(2)}, u32[]{:S(2)}) async-start(f32[1,2,64,2304]{3,1,0,2:T(2,128)} %copy.29), calls=%async_computation | async-start | bytes 2359296 | tf_op jit(solution)/shard_map/all_to_all | solution.py:112
  97.5 21.9 %all-to-all-start.1 = ((f32[1,128,1,768]{3,2,0,1:T(1,128)}), f32[1,128,1,768]{3,2,0,1:T(1,128)S(1)}, u32[]{:S(2)}, u32[]{:S(2)}) async-start(f32[1,128,1,768]{3,2,0,1:T(1,128)} %copy.34), calls=%async_computation.1 | async-start | bytes 786432 | tf_op jit(solution)/shard_map/all_to_all | solution.py:113
  115.2 16.2 %copy-start.2 = (f32[1,2,64,768]{3,2,1,0:T(8,128)S(1)}, f32[1,2,64,768]{3,2,1,0:T(8,128)}, u32[]{:S(2)}) copy-start(f32[1,2,64,768]{3,2,1,0:T(8,128)} %param.9) | copy-start | bytes 1179652
  119.4 38.7 %all-to-all-start.3 = ((f32[1,128,1,2304]{3,2,0,1:T(1,128)}), f32[1,128,1,2304]{3,2,0,1:T(1,128)}, u32[]{:S(2)}, u32[]{:S(2)}) async-start(f32[1,128,1,2304]{3,2,0,1:T(1,128)} %copy.42), calls=%async_computation.3 | async-start | bytes 2359296 | tf_op jit(solution)/shard_map/all_to_all | solution.py:115
  131.3 651.6 %all-reduce.9.cloned.1.call-start = ((), (), s32[]{:S(2)}) async-start(), calls=%async_computation.4 | async-start | bytes 294912 | tf_op jit(solution)/shard_map/psum | solution.py:122
  167.3 214.9 %copy-start.24 = (u32[256]{0:T(256)S(1)}, u32[256]{0:T(256)}, u32[]{:S(2)}) copy-start(u32[256]{0:T(256)} %constant.21) | copy-start | bytes 3076
  357.0 19.3 %collective-permute-start.30 = (f32[16,768]{1,0:T(8,128)}, f32[16,768]{1,0:T(8,128)}, u32[]{:S(2)}, u32[]{:S(2)}) collective-permute-start(f32[16,768]{1,0:T(8,128)} %get-tuple-element.12), channel_id=1, source_target_pairs={{0,60},{4,64},{8,68},{12,72},{16,76},{20,80},{24,84},{28,88},{32,9... | collective-permute-start | bytes 147464
  359.7 14.7 %collective-permute-start.31 = (f32[12,768]{1,0:T(8,128)S(1)}, f32[12,768]{1,0:T(8,128)}, u32[]{:S(2)}, u32[]{:S(2)}) collective-permute-start(f32[12,768]{1,0:T(8,128)S(1)} %slice.19), channel_id=1, source_target_pairs={{0,64},{4,68},{8,72},{12,76},{16,80},{20,84},{24,88},{28,92},{32,9... | collective-permute-start | bytes 110600
  368.7 15.5 %collective-permute-start.29 = (f32[16,768]{1,0:T(8,128)}, f32[16,768]{1,0:T(8,128)}, u32[]{:S(2)}, u32[]{:S(2)}) collective-permute-start(f32[16,768]{1,0:T(8,128)} %get-tuple-element.12), channel_id=1, source_target_pairs={{0,56},{4,60},{8,64},{12,68},{16,72},{20,76},{24,80},{28,84},{32,8... | collective-permute-start | bytes 147464
  370.6 18.3 %collective-permute-start.28 = (f32[16,768]{1,0:T(8,128)}, f32[16,768]{1,0:T(8,128)}, u32[]{:S(2)}, u32[]{:S(2)}) collective-permute-start(f32[16,768]{1,0:T(8,128)} %get-tuple-element.12), channel_id=1, source_target_pairs={{0,52},{4,56},{8,60},{12,64},{16,68},{20,72},{24,76},{28,80},{32,8... | collective-permute-start | bytes 147464
  372.4 17.7 %collective-permute-start.27 = (f32[16,768]{1,0:T(8,128)}, f32[16,768]{1,0:T(8,128)}, u32[]{:S(2)}, u32[]{:S(2)}) collective-permute-start(f32[16,768]{1,0:T(8,128)} %get-tuple-element.12), channel_id=1, source_target_pairs={{0,48},{4,52},{8,56},{12,60},{16,64},{20,68},{24,72},{28,76},{32,8... | collective-permute-start | bytes 147464
  374.3 19.3 %collective-permute-start.26 = (f32[16,768]{1,0:T(8,128)}, f32[16,768]{1,0:T(8,128)}, u32[]{:S(2)}, u32[]{:S(2)}) collective-permute-start(f32[16,768]{1,0:T(8,128)} %get-tuple-element.12), channel_id=1, source_target_pairs={{0,44},{4,48},{8,52},{12,56},{16,60},{20,64},{24,68},{28,72},{32,7... | collective-permute-start | bytes 147464
  376.2 20.5 %collective-permute-start.25 = (f32[16,768]{1,0:T(8,128)}, f32[16,768]{1,0:T(8,128)}, u32[]{:S(2)}, u32[]{:S(2)}) collective-permute-start(f32[16,768]{1,0:T(8,128)} %get-tuple-element.12), channel_id=1, source_target_pairs={{0,40},{4,44},{8,48},{12,52},{16,56},{20,60},{24,64},{28,68},{32,7... | collective-permute-start | bytes 147464
  384.2 20.1 %copy-start.7 = (f32[16,768]{1,0:T(8,128)S(1)}, f32[16,768]{1,0:T(8,128)}, u32[]{:S(2)}) copy-start(f32[16,768]{1,0:T(8,128)} %get-tuple-element.12) | copy-start | bytes 147460
  384.2 20.0 %collective-permute-start.24 = (f32[16,768]{1,0:T(8,128)}, f32[16,768]{1,0:T(8,128)S(1)}, u32[]{:S(2)}, u32[]{:S(2)}) collective-permute-start(f32[16,768]{1,0:T(8,128)} %get-tuple-element.12), channel_id=1, source_target_pairs={{0,36},{4,40},{8,44},{12,48},{16,52},{20,56},{24,60},{28,64},{32,6... | collective-permute-start | bytes 147464
  388.8 17.0 %collective-permute-start.23 = (f32[16,768]{1,0:T(8,128)}, f32[16,768]{1,0:T(8,128)S(1)}, u32[]{:S(2)}, u32[]{:S(2)}) collective-permute-start(f32[16,768]{1,0:T(8,128)} %get-tuple-element.12), channel_id=1, source_target_pairs={{0,32},{4,36},{8,40},{12,44},{16,48},{20,52},{24,56},{28,60},{32,6... | collective-permute-start | bytes 147464
  390.1 19.3 %collective-permute-start.22 = (f32[16,768]{1,0:T(8,128)}, f32[16,768]{1,0:T(8,128)S(1)}, u32[]{:S(2)}, u32[]{:S(2)}) collective-permute-start(f32[16,768]{1,0:T(8,128)} %get-tuple-element.12), channel_id=1, source_target_pairs={{0,28},{4,32},{8,36},{12,40},{16,44},{20,48},{24,52},{28,56},{32,6... | collective-permute-start | bytes 147464
  393.6 20.8 %collective-permute-start.21 = (f32[16,768]{1,0:T(8,128)}, f32[16,768]{1,0:T(8,128)S(1)}, u32[]{:S(2)}, u32[]{:S(2)}) collective-permute-start(f32[16,768]{1,0:T(8,128)} %get-tuple-element.12), channel_id=1, source_target_pairs={{0,24},{4,28},{8,32},{12,36},{16,40},{20,44},{24,48},{28,52},{32,5... | collective-permute-start | bytes 147464
  396.8 18.9 %collective-permute-start.20 = (f32[16,768]{1,0:T(8,128)}, f32[16,768]{1,0:T(8,128)S(1)}, u32[]{:S(2)}, u32[]{:S(2)}) collective-permute-start(f32[16,768]{1,0:T(8,128)} %get-tuple-element.12), channel_id=1, source_target_pairs={{0,20},{4,24},{8,28},{12,32},{16,36},{20,40},{24,44},{28,48},{32,5... | collective-permute-start | bytes 147464
  404.2 11.5 %copy-start.11 = (f32[16,768]{1,0:T(8,128)}, f32[16,768]{1,0:T(8,128)S(1)}, u32[]{:S(2)}) copy-start(f32[16,768]{1,0:T(8,128)S(1)} %collective-permute-done.24) | copy-start | bytes 147460
  404.2 25.0 %collective-permute-start.19 = (f32[16,768]{1,0:T(8,128)S(1)}, f32[16,768]{1,0:T(8,128)S(1)}, u32[]{:S(2)}, u32[]{:S(2)}) collective-permute-start(f32[16,768]{1,0:T(8,128)S(1)} %copy-done.7), channel_id=1, source_target_pairs={{0,16},{4,20},{8,24},{12,28},{16,32},{20,36},{24,40},{28,44},{32,4... | collective-permute-start | bytes 147464
  405.8 9.9 %copy-start.12 = (f32[16,768]{1,0:T(8,128)}, f32[16,768]{1,0:T(8,128)S(1)}, u32[]{:S(2)}) copy-start(f32[16,768]{1,0:T(8,128)S(1)} %collective-permute-done.23) | copy-start | bytes 147460
  405.8 27.9 %collective-permute-start.18 = (f32[16,768]{1,0:T(8,128)S(1)}, f32[16,768]{1,0:T(8,128)S(1)}, u32[]{:S(2)}, u32[]{:S(2)}) collective-permute-start(f32[16,768]{1,0:T(8,128)S(1)} %copy-done.7), channel_id=1, source_target_pairs={{0,12},{4,16},{8,20},{12,24},{16,28},{20,32},{24,36},{28,40},{32,4... | collective-permute-start | bytes 147464
  409.5 6.3 copy-start.13
  409.5 26.2 %collective-permute-start.17 = (f32[16,768]{1,0:T(8,128)S(1)}, f32[16,768]{1,0:T(8,128)S(1)}, u32[]{:S(2)}, u32[]{:S(2)}) collective-permute-start(f32[16,768]{1,0:T(8,128)S(1)} %copy-done.7), channel_id=1, source_target_pairs={{0,8},{4,12},{8,16},{12,20},{16,24},{20,28},{24,32},{28,36},{32,40... | collective-permute-start | bytes 147464
  414.4 23.2 %collective-permute-start.16 = (f32[16,768]{1,0:T(8,128)S(1)}, f32[16,768]{1,0:T(8,128)S(1)}, u32[]{:S(2)}, u32[]{:S(2)}) collective-permute-start(f32[16,768]{1,0:T(8,128)S(1)} %copy-done.7), channel_id=1, source_target_pairs={{0,4},{4,8},{8,12},{12,16},{16,20},{20,24},{24,28},{28,32},{32,36}... | collective-permute-start | bytes 147464
  416.4 23.2 %collective-permute-start.15 = (f32[12,2304]{1,0:T(8,128)S(1)}, f32[12,2304]{1,0:T(8,128)}, u32[]{:S(2)}, u32[]{:S(2)}) collective-permute-start(f32[12,2304]{1,0:T(8,128)S(1)} %slice.18), channel_id=1, source_target_pairs={{0,64},{4,68},{8,72},{12,76},{16,80},{20,84},{24,88},{28,92},{32,9... | collective-permute-start | bytes 331784
  429.3 10.3 %copy-start.16 = (f32[16,768]{1,0:T(8,128)}, f32[16,768]{1,0:T(8,128)S(1)}, u32[]{:S(2)}) copy-start(f32[16,768]{1,0:T(8,128)S(1)} %collective-permute-done.19) | copy-start | bytes 147460
  429.3 165.1 %collective-permute-start.14 = (f32[16,2304]{1,0:T(8,128)}, f32[16,2304]{1,0:T(8,128)}, u32[]{:S(2)}, u32[]{:S(2)}) collective-permute-start(f32[16,2304]{1,0:T(8,128)} %get-tuple-element.11), channel_id=1, source_target_pairs={{0,60},{4,64},{8,68},{12,72},{16,76},{20,80},{24,84},{28,88},{32,9... | collective-permute-start | bytes 442376
  433.7 8.1 %copy-start.17 = (f32[16,768]{1,0:T(8,128)}, f32[16,768]{1,0:T(8,128)S(1)}, u32[]{:S(2)}) copy-start(f32[16,768]{1,0:T(8,128)S(1)} %collective-permute-done.18) | copy-start | bytes 147460
  433.7 162.6 %collective-permute-start.13 = (f32[16,2304]{1,0:T(8,128)}, f32[16,2304]{1,0:T(8,128)}, u32[]{:S(2)}, u32[]{:S(2)}) collective-permute-start(f32[16,2304]{1,0:T(8,128)} %get-tuple-element.11), channel_id=1, source_target_pairs={{0,56},{4,60},{8,64},{12,68},{16,72},{20,76},{24,80},{28,84},{32,8... | collective-permute-start | bytes 442376
  435.6 6.1 copy-start.18
  435.6 162.6 %collective-permute-start.12 = (f32[16,2304]{1,0:T(8,128)}, f32[16,2304]{1,0:T(8,128)}, u32[]{:S(2)}, u32[]{:S(2)}) collective-permute-start(f32[16,2304]{1,0:T(8,128)} %get-tuple-element.11), channel_id=1, source_target_pairs={{0,52},{4,56},{8,60},{12,64},{16,68},{20,72},{24,76},{28,80},{32,8... | collective-permute-start | bytes 442376
  437.6 162.6 %collective-permute-start.11 = (f32[16,2304]{1,0:T(8,128)}, f32[16,2304]{1,0:T(8,128)}, u32[]{:S(2)}, u32[]{:S(2)}) collective-permute-start(f32[16,2304]{1,0:T(8,128)} %get-tuple-element.11), channel_id=1, source_target_pairs={{0,48},{4,52},{8,56},{12,60},{16,64},{20,68},{24,72},{28,76},{32,8... | collective-permute-start | bytes 442376
  439.5 164.7 %collective-permute-start.10 = (f32[16,2304]{1,0:T(8,128)}, f32[16,2304]{1,0:T(8,128)}, u32[]{:S(2)}, u32[]{:S(2)}) collective-permute-start(f32[16,2304]{1,0:T(8,128)} %get-tuple-element.11), channel_id=1, source_target_pairs={{0,44},{4,48},{8,52},{12,56},{16,60},{20,64},{24,68},{28,72},{32,7... | collective-permute-start | bytes 442376
  594.4 17.8 %collective-permute-start.9 = (f32[16,2304]{1,0:T(8,128)}, f32[16,2304]{1,0:T(8,128)}, u32[]{:S(2)}, u32[]{:S(2)}) collective-permute-start(f32[16,2304]{1,0:T(8,128)} %get-tuple-element.11), channel_id=1, source_target_pairs={{0,40},{4,44},{8,48},{12,52},{16,56},{20,60},{24,64},{28,68},{32,7... | collective-permute-start | bytes 442376
  596.3 17.8 %collective-permute-start.8 = (f32[16,2304]{1,0:T(8,128)}, f32[16,2304]{1,0:T(8,128)}, u32[]{:S(2)}, u32[]{:S(2)}) collective-permute-start(f32[16,2304]{1,0:T(8,128)} %get-tuple-element.11), channel_id=1, source_target_pairs={{0,36},{4,40},{8,44},{12,48},{16,52},{20,56},{24,60},{28,64},{32,6... | collective-permute-start | bytes 442376
  598.3 19.8 %collective-permute-start.7 = (f32[16,2304]{1,0:T(8,128)}, f32[16,2304]{1,0:T(8,128)}, u32[]{:S(2)}, u32[]{:S(2)}) collective-permute-start(f32[16,2304]{1,0:T(8,128)} %get-tuple-element.11), channel_id=1, source_target_pairs={{0,32},{4,36},{8,40},{12,44},{16,48},{20,52},{24,56},{28,60},{32,6... | collective-permute-start | bytes 442376
  600.2 20.1 %collective-permute-start.6 = (f32[16,2304]{1,0:T(8,128)}, f32[16,2304]{1,0:T(8,128)}, u32[]{:S(2)}, u32[]{:S(2)}) collective-permute-start(f32[16,2304]{1,0:T(8,128)} %get-tuple-element.11), channel_id=1, source_target_pairs={{0,28},{4,32},{8,36},{12,40},{16,44},{20,48},{24,52},{28,56},{32,6... | collective-permute-start | bytes 442376
  604.2 21.0 %collective-permute-start.5 = (f32[16,2304]{1,0:T(8,128)}, f32[16,2304]{1,0:T(8,128)}, u32[]{:S(2)}, u32[]{:S(2)}) collective-permute-start(f32[16,2304]{1,0:T(8,128)} %get-tuple-element.11), channel_id=1, source_target_pairs={{0,24},{4,28},{8,32},{12,36},{16,40},{20,44},{24,48},{28,52},{32,5... | collective-permute-start | bytes 442376
  612.1 41.7 %collective-permute-start.4 = (f32[16,2304]{1,0:T(8,128)}, f32[16,2304]{1,0:T(8,128)}, u32[]{:S(2)}, u32[]{:S(2)}) collective-permute-start(f32[16,2304]{1,0:T(8,128)} %get-tuple-element.11), channel_id=1, source_target_pairs={{0,20},{4,24},{8,28},{12,32},{16,36},{20,40},{24,44},{28,48},{32,5... | collective-permute-start | bytes 442376
  614.1 39.7 %collective-permute-start.3 = (f32[16,2304]{1,0:T(8,128)}, f32[16,2304]{1,0:T(8,128)}, u32[]{:S(2)}, u32[]{:S(2)}) collective-permute-start(f32[16,2304]{1,0:T(8,128)} %get-tuple-element.11), channel_id=1, source_target_pairs={{0,16},{4,20},{8,24},{12,28},{16,32},{20,36},{24,40},{28,44},{32,4... | collective-permute-start | bytes 442376
  618.1 35.7 %collective-permute-start.2 = (f32[16,2304]{1,0:T(8,128)}, f32[16,2304]{1,0:T(8,128)}, u32[]{:S(2)}, u32[]{:S(2)}) collective-permute-start(f32[16,2304]{1,0:T(8,128)} %get-tuple-element.11), channel_id=1, source_target_pairs={{0,12},{4,16},{8,20},{12,24},{16,28},{20,32},{24,36},{28,40},{32,4... | collective-permute-start | bytes 442376
  620.4 33.5 %collective-permute-start.1 = (f32[16,2304]{1,0:T(8,128)}, f32[16,2304]{1,0:T(8,128)}, u32[]{:S(2)}, u32[]{:S(2)}) collective-permute-start(f32[16,2304]{1,0:T(8,128)} %get-tuple-element.11), channel_id=1, source_target_pairs={{0,8},{4,12},{8,16},{12,20},{16,24},{20,28},{24,32},{28,36},{32,40... | collective-permute-start | bytes 442376
  625.3 28.6 %collective-permute-start = (f32[16,2304]{1,0:T(8,128)}, f32[16,2304]{1,0:T(8,128)}, u32[]{:S(2)}, u32[]{:S(2)}) collective-permute-start(f32[16,2304]{1,0:T(8,128)} %get-tuple-element.11), channel_id=1, source_target_pairs={{0,4},{4,8},{8,12},{12,16},{16,20},{20,24},{24,28},{28,32},{32,36}... | collective-permute-start | bytes 442376
  (14 other events, 33.0 us)
Sparse Core Ops, SparseCore 0:
  684.6 98.2 all-reduce.8
where the time goes:
time: 801 us; the launch traced here: 792 us
  blocking collectives  404 us (50%)
  starting transfers between devices  145 us (18%)
  local copies, waits for them, and re-layouts  89.2 us (11%)
  waiting for transfers between devices  87.3 us (11%)
  matrix products  45.6 us (6%)
  between operations  16.1 us (2%)
    unnamed x2, blocking collectives  341 us
    unnamed x32, starting transfers between devices  100 us
    unnamed x62, local copies, waits for them, and re-layouts  69.6 us
    psum x1, blocking collectives, body(): lax.psum((qkv_rows, out_rows, gain_rows), 'patch')  63.6 us
    psum x1, waiting for transfers between devices, body(): lax.psum((qkv_rows, out_rows, gain_rows), 'patch')  33.9 us
    all_to_all x2, waiting for transfers between devices, body(): lax.all_to_all(value, 'tm', split_axis=2, concat_axis=1, tiled=True)  29.5 us
    all_to_all x2, waiting for transfers between devices, body(): lax.all_to_all(value, 'tm', split_axis=1, concat_axis=2, tiled=True)  23.7 us
    all_to_all x2, starting transfers between devices, body(): lax.all_to_all(value, 'tm', split_axis=2, concat_axis=1, tiled=True)  23.7 us
  transfers between devices with their start and end apart: 37, of which 5 were waited for; matrix products, arithmetic and copies ran while one was open for 9% of the time, Pallas kernels for 0%

commit v1 on v0

v1 whole, which is shorter than its diff:
```python
import functools

import jax
import jax.numpy as jnp
from jax import lax
from jax.experimental import pallas as pl
from jax.experimental.pallas import tpu as pltpu
from jax.sharding import PartitionSpec as P

F32, BF16 = jnp.float32, jnp.bfloat16
MESH = pl.DeviceIdType.MESH


def split(a):
    hi = a.astype(BF16)
    return hi, (a - hi.astype(F32)).astype(BF16)

def dot(a, b, ca=1, cb=0):
    return lax.dot_general(a, b, (((ca,), (cb,)), ((), ())), preferred_element_type=F32)

def rows2(a, b): return jnp.concatenate([a, b], 0)
def cols2(a, b): return jnp.concatenate([a, b], 1)

def product(a_hi, a_lo, b_hi, b_lo, cb=0):
    m = a_hi.shape[0]
    both = dot(rows2(a_hi, a_lo), b_hi, 1, cb)
    return both[:m] + both[m:] + dot(a_hi, b_lo, 1, cb)

def head_pair(x):
    lane = lax.broadcasted_iota(jnp.int32, x.shape, 1)
    first = lane < 64
    return split(rows2(jnp.where(first, x, 0.0), jnp.where(first, 0.0, x)))

def by_heads(x, pair):
    hi, lo = split(x)
    p_hi, p_lo = pair
    return dot(cols2(hi, lo), cols2(p_hi, p_hi), 1, 1) + dot(hi, p_lo, 1, 1)

def mix_heads(x, pair):
    hi, lo = split(x)
    p_hi, p_lo = pair
    both = dot(hi, cols2(p_hi, p_lo))
    return both[:, :128] + both[:, 128:] + dot(lo, p_hi)

def back_heads(x, y):
    hi, lo = split(x.T)
    y_hi, y_lo = split(y)
    both = dot(hi, cols2(y_hi, y_lo))
    r = both[:, :128] + both[:, 128:] + dot(lo, y_hi)
    lane = lax.broadcasted_iota(jnp.int32, (128, 128), 1)
    return jnp.where(lane < 64, r[:128], r[128:])

def prep_weights(w, wh, wl, step):
    for n in range(0, w.shape[1], step):
        hi, lo = split(w[:, n:n + step])
        wh[:, n:n + step] = hi
        wl[:, n:n + step] = lo

def forward(t, gain, wqh, wql, woh, wol, xhat_ref, inv_ref, qkv, probs, mix, out):
    mean = jnp.mean(t, axis=1, keepdims=True)
    cen = t - mean
    inv = lax.rsqrt(jnp.mean(cen * cen, axis=1, keepdims=True) + 1e-5)
    xhat = cen * inv
    xhat_ref[...] = xhat
    inv_ref[...] = jnp.broadcast_to(inv, inv_ref.shape)
    n_hi, n_lo = split(xhat * gain)
    for n in range(0, 2304, 256):
        r = product(n_hi, n_lo, wqh[:, n:n + 256], wql[:, n:n + 256])
        qkv[:, n:n + 256] = r * 0.125 if n < 768 else r
    for p in range(6):
        c = 128 * p
        s = by_heads(qkv[:, c:c + 128], head_pair(qkv[:, 768 + c:768 + c + 128]))
        ps = []
        for h in range(2):
            e = s[:, 128 * h:128 * h + 128]
            e = jnp.exp(e - jnp.max(e, axis=1, keepdims=True))
            ps.append(e / jnp.sum(e, axis=1, keepdims=True))
        pr = cols2(*ps)
        probs[:, 256 * p:256 * p + 256] = pr
        mix[:, c:c + 128] = mix_heads(pr, head_pair(qkv[:, 1536 + c:1536 + c + 128]))
    m_hi, m_lo = split(mix[...])
    for n in range(0, 768, 256):
        out[:, n:n + 256] = t[:, n:n + 256] + product(m_hi, m_lo, woh[:, n:n + 256], wol[:, n:n + 256])

def backward_attn(u, woh, wol, qkv, probs, dmix, dqkv):
    u_hi, u_lo = split(u)
    for n in range(0, 768, 256):
        dmix[:, n:n + 256] = product(u_hi, u_lo, woh[n:n + 256, :], wol[n:n + 256, :], 1)
    for p in range(6):
        c = 128 * p
        do = dmix[:, c:c + 128]
        pr = probs[:, 256 * p:256 * p + 256]
        dqkv[:, 1536 + c:1536 + c + 128] = back_heads(pr, do)
        dp = by_heads(do, head_pair(qkv[:, 1536 + c:1536 + c + 128]))
        ds = []
        for h in range(2):
            a, b = pr[:, 128 * h:128 * h + 128], dp[:, 128 * h:128 * h + 128]
            ds.append(a * (b - jnp.sum(a * b, axis=1, keepdims=True)))
        ds = cols2(*ds)
        dqkv[:, c:c + 128] = 0.125 * mix_heads(ds, head_pair(qkv[:, 768 + c:768 + c + 128]))
        dqkv[:, 768 + c:768 + c + 128] = back_heads(ds, qkv[:, c:c + 128])

def backward_norm(u, gain, wqh, wql, xhat_ref, inv_ref, dqkv, tg):
    d_hi, d_lo = split(dqkv[...])
    for n in range(0, 768, 256):
        tg[:, n:n + 256] = product(d_hi, d_lo, wqh[n:n + 256, :], wql[n:n + 256, :], 1)
    dn = tg[...] * gain
    xhat = xhat_ref[...]
    first = jnp.mean(dn, axis=1, keepdims=True)
    second = jnp.mean(dn * xhat, axis=1, keepdims=True)
    tg[...] = u + inv_ref[:, :1] * (dn - first - xhat * second)

def weight_product(left_t, right, store):
    l_hi, l_lo = left_t
    r_hi, r_lo = right
    lhs = jnp.concatenate([l_hi, l_lo, l_hi], 1)
    rhs = jnp.concatenate([r_hi, r_hi, r_lo], 0)
    store(dot(lhs, rhs))


def place():
    return lax.axis_index("tm"), lax.axis_index("patch")


def pack(value, send):
    for i in range(2):
        for c in range(6):
            send[:, 6 * i + c, :] = value[64 * i:64 * i + 64, 128 * c:128 * c + 128]


def unpack(received, store):
    for i in range(2):
        for c in range(6):
            store(i, c, received[:, 6 * i + c, :])


def greet(extra):
    t, q = place()
    barrier = pltpu.get_barrier_semaphore()

    @pl.loop(1, 64)
    def _(k):
        pl.semaphore_signal(barrier, inc=1, device_id=(t ^ k, q), device_id_type=MESH)

    for peer in extra:
        pl.semaphore_signal(barrier, inc=1, device_id=peer, device_id_type=MESH)
    pl.semaphore_wait(barrier, 63 + len(extra))


def exchange_start(send, received, sems):
    t, q = place()

    @pl.loop(1, 64)
    def _(k):
        peer = lax.rem(t + k, 64)
        pltpu.make_async_remote_copy(
            send.at[peer], received.at[t], sems.at[0], sems.at[1], device_id=(peer, q), device_id_type=MESH
        ).start()

    received[pl.ds(t, 1)] = send[pl.ds(t, 1)]


def exchange_wait(send, received, sems):
    t, q = place()
    all_bytes = pltpu.make_async_remote_copy(
        send.at[pl.ds(0, 63)], received.at[pl.ds(0, 63)], sems.at[0], sems.at[1], device_id=(t ^ 1, q), device_id_type=MESH
    )
    all_bytes.wait_send()
    all_bytes.wait_recv()


def arrive_kernel(tok, up, t_out, u_out, send_t, send_u, recv_t, recv_u, sem_t, sem_u):
    pack(tok, send_t)
    pack(up, send_u)
    greet([])
    exchange_start(send_t, recv_t, sem_t)
    exchange_start(send_u, recv_u, sem_u)
    for recv, send, sem, o in ((recv_t, send_t, sem_t, t_out), (recv_u, send_u, sem_u, u_out)):
        exchange_wait(send, recv, sem)

        def store(i, c, v, o=o):
            o[64 * i:64 * i + 64, 128 * c:128 * c + 128] = v

        unpack(recv, store)


def layer_kernel(t_ref, u_ref, g_ref, wq_ref, wo_ref, out, tg, xhat, mix, dqkv, wrows, wqh, wql, woh, wol, inv, qkv, probs, dmix):
    prep_weights(wq_ref, wqh, wql, 256)
    prep_weights(wo_ref, woh, wol, 256)
    own_rows(wq_ref, wrows)
    forward(t_ref[...], g_ref[...], wqh, wql, woh, wol, xhat, inv, qkv, probs, mix, out)
    backward_attn(u_ref[...], woh, wol, qkv, probs, dmix, dqkv)
    backward_norm(u_ref[...], g_ref[...], wqh, wql, xhat, inv, dqkv, tg)


def own_rows(w_ref, rows):
    t, _ = place()
    base = pl.multiple_of(t // 2 * 24 + lax.rem(t, 2) * 8, 8)
    wide = w_ref[pl.ds(base, 16), :]
    rows[...] = jnp.where(lax.rem(t, 2) == 0, wide[:12], wide[4:])


def bits():
    t, q = place()
    x, yh, yl = lax.rem(t, 4), lax.rem(t // 4, 2), q // 2
    return {"a": lax.rem(x, 2) ^ (x // 2), "b": x // 2, "c": yl ^ yh, "d": yh}


def partner(dim):
    t, q = place()
    return {"a": (t ^ 1, q), "b": (t ^ 3, q), "c": (t, q ^ 2), "d": (t ^ 4, q ^ 2)}[dim]


DIMS = "abcd"
AXIS = {"a": 0, "c": 1, "d": 3, "b": 4}


def order(part):
    return [DIMS[(part + s) % 4] for s in range(4)]


def extents(part, step):
    size = [2, 2, 2, 2, 2]
    for dim in order(part)[:step + 1]:
        size[AXIS[dim]] = 1
    return size


def select(part, step, own, other):
    at = [pl.ds(0, 2), pl.ds(0, 2), pl.ds(2 * part, 2), pl.ds(0, 2), pl.ds(0, 2)]
    for s, dim in enumerate(order(part)[:step + 1]):
        bit = own[dim]
        at[AXIS[dim]] = pl.ds(1 - bit if other and s == step else bit, 1)
    return tuple(at)


def reduce_start(part, step, own, terms, landing, sems):
    copy = pltpu.make_async_remote_copy(
        terms.at[select(part, step, own, True)],
        landing[step][part],
        sems.at[0, step, part],
        sems.at[1, step, part],
        device_id=partner(order(part)[step]),
        device_id_type=MESH,
    )
    copy.start()
    return copy


def reduce_add(part, step, own, terms, landing):
    at = select(part, step, own, False)
    size = extents(part, step)
    buf = landing[step][part]
    for i in range(size[0]):
        for j in range(size[1]):
            for k in range(size[2]):
                for m in range(size[3]):
                    for n in range(size[4]):
                        idx = tuple(s.start + o for s, o in zip(at, (i, j, k, m, n)))
                        terms[idx] = terms[idx] + buf[i, j, k, m, n]


def landing_shapes():
    return [pltpu.VMEM(tuple(extents(part, step)) + (24, 384), F32) for step in range(4) for part in range(4)]


def group_peers():
    t, q = place()
    return [(t ^ dx, q ^ dq) for dx in (0, 1) for dq in range(4) if dx or dq]


def sibling_start(pairs, sems):
    t, q = place()
    copies = []
    for k, (src, dst) in enumerate(pairs):
        copy = pltpu.make_async_remote_copy(src, dst, sems.at[0, k], sems.at[1, k], device_id=(t, q ^ 1), device_id_type=MESH)
        copy.start()
        copies.append(copy)
    return copies


def return_kernel(
    out_in, tg_in, xhat, mix, dqkv, u, g_ref, wrows,
    out, tg, qkv_rows, out_rows, gain_rows,
    send_o, send_g, recv_o, recv_g, terms, s_xhat, s_mix, s_dqkv, s_up, recv_z, own_piece, pieces,
    *rest,
):
    landing = [rest[4 * s:4 * s + 4] for s in range(4)]
    sem_o, sem_g, sem_sib, sem_red, sem_z, sem_p = rest[16:]
    t, q = place()
    core = lax.rem(q, 2)
    own = bits()
    peers = group_peers()
    greet([p for k, p in enumerate(peers) if k != 3] + [(t ^ 4, q ^ 2)])
    theirs, mine = (1 - core) * 1152, core * 1152
    sib = sibling_start(
        [
            (xhat, s_xhat),
            (dqkv.at[:, pl.ds(pl.multiple_of(theirs, 128), 1152)], s_dqkv),
            (mix, s_mix),
            (u.at[:, pl.ds(pl.multiple_of((1 - core) * 384, 128), 384)], s_up),
        ],
        sem_sib,
    )
    pack(out_in, send_o)
    exchange_start(send_o, recv_o, sem_o)
    pack(tg_in, send_g)
    exchange_start(send_g, recv_g, sem_g)
    for copy in sib:
        copy.wait()
    left = split(rows2(xhat[...], s_xhat[...]).T)
    for j in range(4):
        if j < 3:
            col = pl.ds(pl.multiple_of(mine + 384 * j, 128), 384)
            right = split(rows2(dqkv[:, col], s_dqkv[:, 384 * j:384 * j + 384]))
        else:
            left = split(rows2(mix[...], s_mix[...]).T)
            col = pl.ds(pl.multiple_of(core * 384, 128), 384)
            right = split(rows2(u[:, col], s_up[...]))

        def store(v, j=j):
            terms[j // 2, j % 2] = v.reshape(8, 2, 2, 24, 384)

        weight_product(left, right, store)
    for step in range(4):
        copies = [reduce_start(p, step, own, terms, landing, sem_red) for p in range(4)]
        for p in range(4):
            copies[p].wait()
            reduce_add(p, step, own, terms, landing)
    z = t // 8
    held = terms.at[own["a"], own["c"], :, own["d"], own["b"]]

    @pl.loop(1, 8)
    def _(k):
        pz = z ^ k
        pltpu.make_async_remote_copy(
            held.at[pz], recv_z.at[z], sem_z.at[0], sem_z.at[1], device_id=(t ^ (8 * k), q), device_id_type=MESH
        ).start()

    recv_z[pl.ds(z, 1)] = held[pl.ds(z, 1)]
    every = pltpu.make_async_remote_copy(
        recv_z.at[pl.ds(0, 7)], recv_z.at[pl.ds(0, 7)], sem_z.at[0], sem_z.at[1], device_id=(t ^ 8, q), device_id_type=MESH
    )
    every.wait_send()
    every.wait_recv()
    total = recv_z[0]
    for k in range(1, 8):
        total = total + recv_z[k]
    own_piece[0] = total[:12]
    own_piece[1] = total[12:]
    me = core * 4 + own["a"] * 2 + own["c"]
    copies = []
    for k, (pt, pq) in enumerate(peers):
        copy = pltpu.make_async_remote_copy(
            own_piece.at[lax.rem(pt, 2)], pieces.at[me], sem_p.at[0, k], sem_p.at[1, k], device_id=(pt, pq), device_id_type=MESH
        )
        copy.start()
        copies.append(copy)
    pieces[pl.ds(me, 1)] = own_piece[pl.ds(lax.rem(t, 2), 1)]
    for copy in copies:
        copy.wait()
    lane = lax.broadcasted_iota(jnp.int32, (12, 768), 1)
    row = lax.broadcasted_iota(jnp.int32, (12, 768), 0)
    gain = jnp.sum(jnp.where(lane == row + 12 * t, g_ref[...], 0.0), axis=1, keepdims=True)
    gain_sum = jnp.zeros((12, 1), F32)
    for k in range(8):
        j, c = k % 4, k // 4
        piece = pieces[k]
        if j < 3:
            col = 1152 * c + 384 * j
            qkv_rows[:, col:col + 384] = piece * gain
            gain_sum = gain_sum + jnp.sum(piece * wrows[:, col:col + 384], axis=1, keepdims=True)
        else:
            out_rows[:, 384 * c:384 * c + 384] = piece
    gain_rows[...] = jnp.broadcast_to(gain_sum, (12, 128))
    for send, recv, sem, o in ((send_o, recv_o, sem_o, out), (send_g, recv_g, sem_g, tg)):
        exchange_wait(send, recv, sem)

        def store(i, c, v, o=o):
            o[64 * i:64 * i + 64, 128 * c:128 * c + 128] = v

        unpack(recv, store)


def body(tokens, norm_gain_vector, qkv_weight, out_weight, upstream):
    shape = tokens.shape
    tok, up = tokens.reshape(128, 768), upstream.reshape(128, 768)
    gain = norm_gain_vector.reshape(1, 768)
    vmem = pl.BlockSpec(memory_space=pltpu.VMEM)
    S = lambda *s: jax.ShapeDtypeStruct(s, F32)
    V = lambda *s: pltpu.VMEM(s, F32)
    H = lambda *s: pltpu.VMEM(s, BF16)
    D = lambda *s: pltpu.SemaphoreType.DMA(s)
    big = 56 * 2 ** 20
    t_in, u_in = pl.pallas_call(
        arrive_kernel,
        out_shape=[S(128, 768)] * 2,
        in_specs=[vmem] * 2,
        out_specs=[vmem] * 2,
        scratch_shapes=[V(64, 12, 128)] * 4 + [D(2), D(2)],
        compiler_params=pltpu.CompilerParams(collective_id=0, has_side_effects=True, vmem_limit_bytes=big),
    )(tok, up)
    out_in, tg_in, xhat, mix, dqkv, wrows = pl.pallas_call(
        layer_kernel,
        out_shape=[S(128, 768), S(128, 768), S(128, 768), S(128, 768), S(128, 2304), S(12, 2304)],
        in_specs=[vmem] * 5,
        out_specs=[vmem] * 6,
        scratch_shapes=[
            H(768, 2304), H(768, 2304), H(768, 768), H(768, 768),
            V(128, 128), V(128, 2304), V(128, 1536), V(128, 768),
        ],
        compiler_params=pltpu.CompilerParams(vmem_limit_bytes=big),
    )(t_in, u_in, gain, qkv_weight, out_weight)
    out, tg, qkv_rows, out_rows, gain_rows = pl.pallas_call(
        return_kernel,
        out_shape=[S(128, 768), S(128, 768), S(12, 2304), S(12, 768), S(12, 128)],
        in_specs=[vmem] * 8,
        out_specs=[vmem] * 5,
        scratch_shapes=[V(64, 12, 128)] * 4
        + [V(2, 2, 8, 2, 2, 24, 384), V(128, 768), V(128, 768), V(128, 1152), V(128, 384), V(8, 24, 384), V(2, 12, 384), V(8, 12, 384)]
        + landing_shapes()
        + [D(2), D(2), D(2, 4), D(2, 4, 4), D(2), D(2, 7)],
        compiler_params=pltpu.CompilerParams(collective_id=1, has_side_effects=True, vmem_limit_bytes=big),
    )(out_in, tg_in, xhat, mix, dqkv, u_in, gain, wrows)
    return out.reshape(shape), tg.reshape(shape), qkv_rows, out_rows, gain_rows[:, 0]


def solution(mesh):
    whole = P(None, "tm", "patch", None)
    rows = P("tm", None)
    return jax.shard_map(
        body,
        mesh=mesh,
        in_specs=(whole, P(), P(), P(), whole),
        out_specs=(whole, whole, rows, rows, P("tm")),
        check_vma=False,
    )
```

time: 801 us -> 128 us (0.16); the launches traced: 792 us -> 128 us
  blocking collectives: 404 us -> 0 us
  starting transfers between devices: 145 us -> 0 us
  Pallas kernels: 0 us -> 118 us
  waiting for transfers between devices: 87.3 us -> 0 us
  local copies, waits for them, and re-layouts: 89.2 us -> 9.12 us
  matrix products: 45.6 us -> 0 us
  between operations: 16.1 us -> 0.65 us
    unnamed x2 -> x0, blocking collectives: 341 us -> none
    pallas_call x0 -> x3, Pallas kernels: none -> 118 us  [the longest x1 69.7 us: body(): pl.pallas_call(return_kernel, out_shape=[S(128, 768), S(128, 768), S(12,...]
    unnamed x32 -> x0, starting transfers between devices: 100 us -> none
    psum x1 -> x0, blocking collectives: 63.6 us -> none  [body(): lax.psum((qkv_rows, out_rows, gain_rows), 'patch')]
    unnamed x62 -> x4, local copies, waits for them, and re-layouts: 69.6 us -> 6.53 us
    all_to_all x4 -> x0, waiting for transfers between devices: 53.3 us -> none  [the longest x2 29.5 us: body(): lax.all_to_all(value, 'tm', split_axis=2, concat_axis=1, tiled=True)]
    dot_general x12 -> x0, matrix products: 45.6 us -> none  [the longest x4 22.8 us: project(): return jnp.einsum('bfpd,de->bfpe', left, weight, precision=HIGH)]
    all_to_all x4 -> x0, starting transfers between devices: 44.9 us -> none  [the longest x2 23.7 us: body(): lax.all_to_all(value, 'tm', split_axis=2, concat_axis=1, tiled=True)]
  transfers between devices with their start and end apart: 37 -> 0, of which waited for: 5 -> 0; matrix products, arithmetic and copies ran while one was open for 9% -> 0% of each run, Pallas kernels for 0% -> 0%
where the time goes in v1:
time: 128 us
  Pallas kernels  118 us (92%)
  local copies, waits for them, and re-layouts  9.12 us (7%)
    pallas_call x1, Pallas kernels, body(): pl.pallas_call(return_kernel, out_shape=[S(128, 768), S(128, 768), S(12,...  69.7 us
    pallas_call x1, Pallas kernels, body(): pl.pallas_call(arrive_kernel, out_shape=[S(128, 768)] * 2, in_specs=[vmem...  32.6 us
    pallas_call x1, Pallas kernels, body(): pl.pallas_call(layer_kernel, out_shape=[S(128, 768), S(128, 768), S(128,...  15.7 us
    unnamed x4, local copies, waits for them, and re-layouts  6.53 us

profile of v1, /device:TPU:1, one launch (start us, length us, event | category | flops | bytes accessed | tf_op | source)
XLA Modules:
  0.0 127.7 jit_solution(8940689494463888505)
XLA Ops:
  0.6 1.3 reshape.27.g_ref
  1.9 32.6 %shard_map.92 = (f32[128,768]{1,0:T(8,128)}, f32[128,768]{1,0:T(8,128)}) custom-call(f32[128,768]{1,0:T(8,128)} %bitcast.4, f32[128,768]{1,0:T(8,128)} %bitcast.5), custom_call_target="tpu_custom_call" | custom-call | tf_op jit(solution)/shard_map/pallas_call | solution.py:395
  34.5 15.7 %shard_map.93 = (f32[128,768]{1,0:T(8,128)}, f32[128,768]{1,0:T(8,128)}, f32[128,768]{1,0:T(8,128)}, f32[128,768]{1,0:T(8,128)}, f32[128,2304]{1,0:T(8,128)}, /*index=5*/f32[12,2304]{1,0:T(8,128)}) custom-call(f32[128,768]{1,0:T(8,128)} %get-tuple-element.18.t_ref, f32[128,768]{1,0:T(8,128)} %get-tuple-element.19.u_ref.u, f32[1,768]{1,0:T(1,128)} %reshape.27.g_ref, ...), custom_call_target="tpu_custom_call" | custom-call | tf_op jit(solution)/shard_map/pallas_call | solution.py:403
  50.2 69.7 %shard_map.94 = (f32[128,768]{1,0:T(8,128)}, f32[128,768]{1,0:T(8,128)}, f32[12,2304]{1,0:T(8,128)}, f32[12,768]{1,0:T(8,128)}, f32[12,128]{1,0:T(8,128)}) custom-call(f32[128,768]{1,0:T(8,128)} %get-tuple-element.20.out_in, f32[128,768]{1,0:T(8,128)} %get-tuple-element.21.tg_in, f32[128,768]{1,0:T(8,128)} %get-tuple-element.22.xhat, ...), custom_call_target="tpu_custom_call" | custom-call | tf_op jit(solution)/shard_map/pallas_call | solution.py:414
  119.9 1.3 %slice_reduce_fusion = f32[12]{0:T(128)} fusion(f32[12,128]{1,0:T(8,128)} %get-tuple-element.30), kind=kLoop, calls=%fused_computation | loop fusion | bytes 96 | tf_op jit(solution)/shard_map/slice | solution.py:425
  121.2 1.8 %copy.14 = f32[1,2,64,768]{3,2,1,0:T(8,128)} copy(f32[1,2,64,768]{3,2,1,0:T(8,128)} %bitcast.7) | data formatting | bytes 786432
  123.0 1.8 %copy.15 = f32[1,2,64,768]{3,2,1,0:T(8,128)} copy(f32[1,2,64,768]{3,2,1,0:T(8,128)} %bitcast.6) | data formatting | bytes 786432
  124.7 1.6 %copy.16 = f32[12,2304]{1,0:T(8,128)} copy(f32[12,2304]{1,0:T(8,128)} %get-tuple-element.38) | data formatting | bytes 221184
  126.3 1.4 %copy.17 = f32[12,768]{1,0:T(8,128)} copy(f32[12,768]{1,0:T(8,128)} %get-tuple-element.39) | data formatting | bytes 73728

commit v2 on v1

--- a/solution.py
+++ b/solution.py
@@ -110,14 +110,6 @@
     second = jnp.mean(dn * xhat, axis=1, keepdims=True)
     tg[...] = u + inv_ref[:, :1] * (dn - first - xhat * second)
 
-def weight_product(left_t, right, store):
-    l_hi, l_lo = left_t
-    r_hi, r_lo = right
-    lhs = jnp.concatenate([l_hi, l_lo, l_hi], 1)
-    rhs = jnp.concatenate([r_hi, r_hi, r_lo], 0)
-    store(dot(lhs, rhs))
-
-
 def place():
     return lax.axis_index("tm"), lax.axis_index("patch")
 
@@ -144,7 +136,10 @@
 
     for peer in extra:
         pl.semaphore_signal(barrier, inc=1, device_id=peer, device_id_type=MESH)
-    pl.semaphore_wait(barrier, 63 + len(extra))
+
+
+def greeted(extra):
+    pl.semaphore_wait(pltpu.get_barrier_semaphore(), 63 + len(extra))
 
 
 def exchange_start(send, received, sems):
@@ -169,30 +164,6 @@
     all_bytes.wait_recv()
 
 
-def arrive_kernel(tok, up, t_out, u_out, send_t, send_u, recv_t, recv_u, sem_t, sem_u):
-    pack(tok, send_t)
-    pack(up, send_u)
-    greet([])
-    exchange_start(send_t, recv_t, sem_t)
-    exchange_start(send_u, recv_u, sem_u)
-    for recv, send, sem, o in ((recv_t, send_t, sem_t, t_out), (recv_u, send_u, sem_u, u_out)):
-        exchange_wait(send, recv, sem)
-
-        def store(i, c, v, o=o):
-            o[64 * i:64 * i + 64, 128 * c:128 * c + 128] = v
-
-        unpack(recv, store)
-
-
-def layer_kernel(t_ref, u_ref, g_ref, wq_ref, wo_ref, out, tg, xhat, mix, dqkv, wrows, wqh, wql, woh, wol, inv, qkv, probs, dmix):
-    prep_weights(wq_ref, wqh, wql, 256)
-    prep_weights(wo_ref, woh, wol, 256)
-    own_rows(wq_ref, wrows)
-    forward(t_ref[...], g_ref[...], wqh, wql, woh, wol, xhat, inv, qkv, probs, mix, out)
-    backward_attn(u_ref[...], woh, wol, qkv, probs, dmix, dqkv)
-    backward_norm(u_ref[...], g_ref[...], wqh, wql, xhat, inv, dqkv, tg)
-
-
 def own_rows(w_ref, rows):
     t, _ = place()
     base = pl.multiple_of(t // 2 * 24 + lax.rem(t, 2) * 8, 8)
@@ -213,29 +184,30 @@
 
 DIMS = "abcd"
 AXIS = {"a": 0, "c": 1, "d": 3, "b": 4}
+PARTS = (0, 1, 4, 5, 2, 3, 6, 7)
 
 
 def order(part):
-    return [DIMS[(part + s) % 4] for s in range(4)]
+    return [DIMS[(part // 2 + s) % 4] for s in range(4)]
 
 
 def extents(part, step):
-    size = [2, 2, 2, 2, 2]
+    size = [2, 2, 1, 2, 2]
     for dim in order(part)[:step + 1]:
         size[AXIS[dim]] = 1
     return size
 
 
 def select(part, step, own, other):
-    at = [pl.ds(0, 2), pl.ds(0, 2), pl.ds(2 * part, 2), pl.ds(0, 2), pl.ds(0, 2)]
+    at = [pl.ds(0, 2), pl.ds(0, 2), pl.ds(part, 1), pl.ds(0, 2), pl.ds(0, 2)]
     for s, dim in enumerate(order(part)[:step + 1]):
         bit = own[dim]
         at[AXIS[dim]] = pl.ds(1 - bit if other and s == step else bit, 1)
     return tuple(at)
 
 
-def reduce_start(part, step, own, terms, landing, sems):
-    copy = pltpu.make_async_remote_copy(
+def reduce_copy(part, step, own, terms, landing, sems):
+    return pltpu.make_async_remote_copy(
         terms.at[select(part, step, own, True)],
         landing[step][part],
         sems.at[0, step, part],
@@ -243,8 +215,6 @@
         device_id=partner(order(part)[step]),
         device_id_type=MESH,
     )
-    copy.start()
-    return copy
 
 
 def reduce_add(part, step, own, terms, landing):
@@ -261,7 +231,7 @@
 
 
 def landing_shapes():
-    return [pltpu.VMEM(tuple(extents(part, step)) + (24, 384), F32) for step in range(4) for part in range(4)]
+    return [pltpu.VMEM(tuple(extents(part, step)) + (24, 384), F32) for step in range(4) for part in range(8)]
 
 
 def group_peers():
@@ -269,75 +239,139 @@
     return [(t ^ dx, q ^ dq) for dx in (0, 1) for dq in range(4) if dx or dq]
 
 
-def sibling_start(pairs, sems):
-    t, q = place()
-    copies = []
-    for k, (src, dst) in enumerate(pairs):
-        copy = pltpu.make_async_remote_copy(src, dst, sems.at[0, k], sems.at[1, k], device_id=(t, q ^ 1), device_id_type=MESH)
-        copy.start()
-        copies.append(copy)
-    return copies
-
-
-def return_kernel(
-    out_in, tg_in, xhat, mix, dqkv, u, g_ref, wrows,
-    out, tg, qkv_rows, out_rows, gain_rows,
-    send_o, send_g, recv_o, recv_g, terms, s_xhat, s_mix, s_dqkv, s_up, recv_z, own_piece, pieces,
+def sibling_copy(src, dst, sems, k):
+    t, q = place()
+    return pltpu.make_async_remote_copy(src, dst, sems.at[0, k], sems.at[1, k], device_id=(t, q ^ 1), device_id_type=MESH)
+
+
+def join_left(ref, j, own, theirs):
+    hi, lo = split(rows2(own, theirs).T)
+    ref[j, :, :256] = hi
+    ref[j, :, 256:512] = lo
+    ref[j, :, 512:] = hi
+
+
+def join_right(ref, j, own, theirs):
+    hi, lo = split(rows2(own, theirs))
+    ref[j, :256] = hi
+    ref[j, 256:512] = hi
+    ref[j, 512:] = lo
+
+
+def layer_kernel(
+    tok_hbm, up_hbm, g_ref, wq_hbm, wo_hbm,
+    o_hbm, g_hbm, p_hbm, w_hbm,
+    tok, wq, wo, wrows, up,
+    wqh, wql, woh, wol, t_ref, u_ref, out, tg, xhat, inv, qkv, probs, mix, dmix, dqkv,
+    send_t, send_u, send_o, send_g, recv_t, recv_u, recv_o, recv_g,
+    s_xhat, s_mix, s_dqkv, s_up, left, right, terms, recv_z, own_piece, pieces,
     *rest,
 ):
-    landing = [rest[4 * s:4 * s + 4] for s in range(4)]
-    sem_o, sem_g, sem_sib, sem_red, sem_z, sem_p = rest[16:]
-    t, q = place()
-    core = lax.rem(q, 2)
+    landing = [rest[8 * s:8 * s + 8] for s in range(4)]
+    sem_in, sem_t, sem_u, sem_o, sem_g, sem_sib, sem_red, sem_z, sem_p, sem_out = rest[32:]
+    t, q = place()
+    z, core = t // 8, lax.rem(q, 2)
     own = bits()
     peers = group_peers()
-    greet([p for k, p in enumerate(peers) if k != 3] + [(t ^ 4, q ^ 2)])
-    theirs, mine = (1 - core) * 1152, core * 1152
-    sib = sibling_start(
-        [
-            (xhat, s_xhat),
-            (dqkv.at[:, pl.ds(pl.multiple_of(theirs, 128), 1152)], s_dqkv),
-            (mix, s_mix),
-            (u.at[:, pl.ds(pl.multiple_of((1 - core) * 384, 128), 384)], s_up),
-        ],
-        sem_sib,
-    )
-    pack(out_in, send_o)
+    extra = [p for k, p in enumerate(peers) if k != 3] + [(t ^ 4, q ^ 2)]
+    loads = [
+        pltpu.make_async_copy(src, dst, sem_in.at[k])
+        for k, (src, dst) in enumerate(((tok_hbm, tok), (up_hbm, up), (wq_hbm, wq), (wo_hbm, wo)))
+    ]
+    for load in loads:
+        load.start()
+    greet(extra)
+    loads[0].wait()
+    pack(tok, send_t)
+    greeted(extra)
+    exchange_start(send_t, recv_t, sem_t)
+    loads[1].wait()
+    pack(up, send_u)
+    exchange_start(send_u, recv_u, sem_u)
+    loads[2].wait()
+    prep_weights(wq, wqh, wql, 256)
+    own_rows(wq, wrows)
+    loads[3].wait()
+    prep_weights(wo, woh, wol, 256)
+    gain = g_ref[...].reshape(1, 768)
+
+    def into(ref):
+        def store(i, c, v):
+            ref[64 * i:64 * i + 64, 128 * c:128 * c + 128] = v
+
+        return store
+
+    exchange_wait(send_t, recv_t, sem_t)
+    unpack(recv_t, into(t_ref))
+    forward(t_ref[...], gain, wqh, wql, woh, wol, xhat, inv, qkv, probs, mix, out)
+    sib = [sibling_copy(xhat, s_xhat, sem_sib, 0), sibling_copy(mix, s_mix, sem_sib, 1)]
+    for copy in sib:
+        copy.start()
+    pack(out, send_o)
     exchange_start(send_o, recv_o, sem_o)
-    pack(tg_in, send_g)
+    for k, (a, b) in enumerate(((xhat, s_xhat), (mix, s_mix))):
+        sib[k].wait()
+        join_left(left, k, a[...], b[...])
+    exchange_wait(send_u, recv_u, sem_u)
+    unpack(recv_u, into(u_ref))
+    sib_u = sibling_copy(u_ref.at[:, pl.ds(pl.multiple_of((1 - core) * 384, 128), 384)], s_up, sem_sib, 2)
+    sib_u.start()
+    backward_attn(u_ref[...], woh, wol, qkv, probs, dmix, dqkv)
+    sib_d = sibling_copy(dqkv.at[:, pl.ds(pl.multiple_of((1 - core) * 1152, 128), 1152)], s_dqkv, sem_sib, 3)
+    sib_d.start()
+    backward_norm(u_ref[...], gain, wqh, wql, xhat, inv, dqkv, tg)
+    sib_u.wait()
+    join_right(right, 3, u_ref[:, pl.ds(pl.multiple_of(core * 384, 128), 384)], s_up[...])
+    sib_d.wait()
+    for j in range(3):
+        col = pl.ds(pl.multiple_of(core * 1152 + 384 * j, 128), 384)
+        join_right(right, j, dqkv[:, col], s_dqkv[:, 384 * j:384 * j + 384])
+
+    def block(r, i, j):
+        g = 2 * i + j
+        v = dot(left[g // 3, 192 * r:192 * r + 192, :], right[g])
+        terms[i, j, 2 * r:2 * r + 2] = v.reshape(2, 2, 2, 24, 384)
+
+    def begin(p, step):
+        reduce_copy(p, step, own, terms, landing, sem_red).start()
+
+    a, c = own["a"], own["c"]
+    both = (0, 1)
+    for r, blocks in ((0, [(1 - a, j) for j in both]), (2, [(i, 1 - c) for i in both]), (1, None), (3, None)):
+        for i, j in blocks or [(i, j) for i in both for j in both]:
+            block(r, i, j)
+        begin(2 * r, 0)
+        begin(2 * r + 1, 0)
+    for j in both:
+        block(0, a, j)
+    for i in both:
+        block(2, i, c)
+    pack(tg, send_g)
     exchange_start(send_g, recv_g, sem_g)
-    for copy in sib:
-        copy.wait()
-    left = split(rows2(xhat[...], s_xhat[...]).T)
-    for j in range(4):
-        if j < 3:
-            col = pl.ds(pl.multiple_of(mine + 384 * j, 128), 384)
-            right = split(rows2(dqkv[:, col], s_dqkv[:, 384 * j:384 * j + 384]))
-        else:
-            left = split(rows2(mix[...], s_mix[...]).T)
-            col = pl.ds(pl.multiple_of(core * 384, 128), 384)
-            right = split(rows2(u[:, col], s_up[...]))
-
-        def store(v, j=j):
-            terms[j // 2, j % 2] = v.reshape(8, 2, 2, 24, 384)
-
-        weight_product(left, right, store)
     for step in range(4):
-        copies = [reduce_start(p, step, own, terms, landing, sem_red) for p in range(4)]
-        for p in range(4):
-            copies[p].wait()
+        for p in PARTS:
+            reduce_copy(p, step, own, terms, landing, sem_red).wait()
             reduce_add(p, step, own, terms, landing)
-    z = t // 8
-    held = terms.at[own["a"], own["c"], :, own["d"], own["b"]]
-
-    @pl.loop(1, 8)
-    def _(k):
-        pz = z ^ k
-        pltpu.make_async_remote_copy(
-            held.at[pz], recv_z.at[z], sem_z.at[0], sem_z.at[1], device_id=(t ^ (8 * k), q), device_id_type=MESH
-        ).start()
-
-    recv_z[pl.ds(z, 1)] = held[pl.ds(z, 1)]
+            if step < 3:
+                begin(p, step + 1)
+            else:
+
+                @pl.when(z != p)
+                def _(p=p):
+                    pltpu.make_async_remote_copy(
+                        terms.at[a, c, p, own["d"], own["b"]], recv_z.at[z], sem_z.at[0], sem_z.at[1],
+                        device_id=(p * 8 + lax.rem(t, 8), q), device_id_type=MESH,
+                    ).start()
+
+    recv_z[pl.ds(z, 1)] = terms[a, c, pl.ds(z, 1), own["d"], own["b"]]
+    exchange_wait(send_o, recv_o, sem_o)
+    exchange_wait(send_g, recv_g, sem_g)
+    results = [
+        pltpu.make_async_copy(src, dst, sem_out.at[k])
+        for k, (src, dst) in enumerate(((recv_o, o_hbm), (recv_g, g_hbm), (wrows, w_hbm), (pieces, p_hbm)))
+    ]
+    for result in results[:3]:
+        result.start()
     every = pltpu.make_async_remote_copy(
         recv_z.at[pl.ds(0, 7)], recv_z.at[pl.ds(0, 7)], sem_z.at[0], sem_z.at[1], device_id=(t ^ 8, q), device_id_type=MESH
     )
@@ -348,7 +382,7 @@
         total = total + recv_z[k]
     own_piece[0] = total[:12]
     own_piece[1] = total[12:]
-    me = core * 4 + own["a"] * 2 + own["c"]
+    me = core * 4 + a * 2 + c
     copies = []
     for k, (pt, pq) in enumerate(peers):
         copy = pltpu.make_async_remote_copy(
@@ -359,9 +393,16 @@
     pieces[pl.ds(me, 1)] = own_piece[pl.ds(lax.rem(t, 2), 1)]
     for copy in copies:
         copy.wait()
+    results[3].start()
+    for result in results:
+        result.wait()
+
+
+def finish_kernel(recv_o, recv_g, pieces, wrows, g_ref, out, tg, qkv_rows, out_rows, gain_rows):
+    t, _ = place()
     lane = lax.broadcasted_iota(jnp.int32, (12, 768), 1)
     row = lax.broadcasted_iota(jnp.int32, (12, 768), 0)
-    gain = jnp.sum(jnp.where(lane == row + 12 * t, g_ref[...], 0.0), axis=1, keepdims=True)
+    gain = jnp.sum(jnp.where(lane == row + 12 * t, g_ref[...].reshape(1, 768), 0.0), axis=1, keepdims=True)
     gain_sum = jnp.zeros((12, 1), F32)
     for k in range(8):
         j, c = k % 4, k // 4
@@ -372,9 +413,8 @@
             gain_sum = gain_sum + jnp.sum(piece * wrows[:, col:col + 384], axis=1, keepdims=True)
         else:
             out_rows[:, 384 * c:384 * c + 384] = piece
-    gain_rows[...] = jnp.broadcast_to(gain_sum, (12, 128))
-    for send, recv, sem, o in ((send_o, recv_o, sem_o, out), (send_g, recv_g, sem_g, tg)):
-        exchange_wait(send, recv, sem)
+    gain_rows[...] = gain_sum.reshape(12)
+    for recv, o in ((recv_o, out), (recv_g, tg)):
 
         def store(i, c, v, o=o):
             o[64 * i:64 * i + 64, 128 * c:128 * c + 128] = v
@@ -385,44 +425,36 @@
 def body(tokens, norm_gain_vector, qkv_weight, out_weight, upstream):
     shape = tokens.shape
     tok, up = tokens.reshape(128, 768), upstream.reshape(128, 768)
-    gain = norm_gain_vector.reshape(1, 768)
-    vmem = pl.BlockSpec(memory_space=pltpu.VMEM)
+    vmem, hbm = pl.BlockSpec(memory_space=pltpu.VMEM), pl.BlockSpec(memory_space=pl.ANY)
     S = lambda *s: jax.ShapeDtypeStruct(s, F32)
     V = lambda *s: pltpu.VMEM(s, F32)
     H = lambda *s: pltpu.VMEM(s, BF16)
     D = lambda *s: pltpu.SemaphoreType.DMA(s)
-    big = 56 * 2 ** 20
-    t_in, u_in = pl.pallas_call(
-        arrive_kernel,
-        out_shape=[S(128, 768)] * 2,
-        in_specs=[vmem] * 2,
-        out_specs=[vmem] * 2,
-        scratch_shapes=[V(64, 12, 128)] * 4 + [D(2), D(2)],
-        compiler_params=pltpu.CompilerParams(collective_id=0, has_side_effects=True, vmem_limit_bytes=big),
-    )(tok, up)
-    out_in, tg_in, xhat, mix, dqkv, wrows = pl.pallas_call(
+    rows = V(128, 768)
+    pack_buffer = V(64, 12, 128)
+    recv_o, recv_g, pieces, wrows = pl.pallas_call(
         layer_kernel,
-        out_shape=[S(128, 768), S(128, 768), S(128, 768), S(128, 768), S(128, 2304), S(12, 2304)],
+        out_shape=[S(64, 12, 128), S(64, 12, 128), S(8, 12, 384), S(12, 2304)],
+        in_specs=[hbm, hbm, vmem, hbm, hbm],
+        out_specs=[hbm] * 4,
+        scratch_shapes=[rows, V(768, 2304), V(768, 768), V(12, 2304), rows]
+        + [H(768, 2304), H(768, 2304), H(768, 768), H(768, 768)]
+        + [rows, rows, rows, rows, rows, V(128, 128), V(128, 2304), V(128, 1536), rows, rows, V(128, 2304)]
+        + [pack_buffer] * 8
+        + [rows, rows, V(128, 1152), V(128, 384), H(2, 768, 768), H(4, 768, 384)]
+        + [V(2, 2, 8, 2, 2, 24, 384), V(8, 24, 384), V(2, 12, 384), V(8, 12, 384)]
+        + landing_shapes()
+        + [D(4), D(2), D(2), D(2), D(2), D(2, 4), D(2, 4, 8), D(2), D(2, 7), D(4)],
+        compiler_params=pltpu.CompilerParams(collective_id=0, has_side_effects=True, vmem_limit_bytes=60 * 2 ** 20),
+    )(tok, up, norm_gain_vector, qkv_weight, out_weight)
+    out, tg, qkv_rows, out_rows, gain_rows = pl.pallas_call(
+        finish_kernel,
+        out_shape=[S(128, 768), S(128, 768), S(12, 2304), S(12, 768), S(12)],
         in_specs=[vmem] * 5,
-        out_specs=[vmem] * 6,
-        scratch_shapes=[
-            H(768, 2304), H(768, 2304), H(768, 768), H(768, 768),
-            V(128, 128), V(128, 2304), V(128, 1536), V(128, 768),
-        ],
-        compiler_params=pltpu.CompilerParams(vmem_limit_bytes=big),
-    )(t_in, u_in, gain, qkv_weight, out_weight)
-    out, tg, qkv_rows, out_rows, gain_rows = pl.pallas_call(
-        return_kernel,
-        out_shape=[S(128, 768), S(128, 768), S(12, 2304), S(12, 768), S(12, 128)],
-        in_specs=[vmem] * 8,
         out_specs=[vmem] * 5,
-        scratch_shapes=[V(64, 12, 128)] * 4
-        + [V(2, 2, 8, 2, 2, 24, 384), V(128, 768), V(128, 768), V(128, 1152), V(128, 384), V(8, 24, 384), V(2, 12, 384), V(8, 12, 384)]
-        + landing_shapes()
-        + [D(2), D(2), D(2, 4), D(2, 4, 4), D(2), D(2, 7)],
-        compiler_params=pltpu.CompilerParams(collective_id=1, has_side_effects=True, vmem_limit_bytes=big),
-    )(out_in, tg_in, xhat, mix, dqkv, u_in, gain, wrows)
-    return out.reshape(shape), tg.reshape(shape), qkv_rows, out_rows, gain_rows[:, 0]
+        compiler_params=pltpu.CompilerParams(vmem_limit_bytes=16 * 2 ** 20),
+    )(recv_o, recv_g, pieces, wrows, norm_gain_vector)
+    return out.reshape(shape), tg.reshape(shape), qkv_rows, out_rows, gain_rows
 
 
 def solution(mesh):

time: 128 us -> 95.1 us (0.74)
  Pallas kernels: 118 us -> 90.3 us
  local copies, waits for them, and re-layouts: 9.12 us -> 3.92 us
    pallas_call x3 -> x2, Pallas kernels: 118 us -> 90.3 us  [the longest x1 89 us: body(): pl.pallas_call(layer_kernel, out_shape=[S(64, 12, 128), S(64, 12, 128), S...]
    unnamed x4 -> x10, local copies, waits for them, and re-layouts: 6.53 us -> 3.92 us
    slice x1 -> x0, local copies, waits for them, and re-layouts: 1.32 us -> none  [body(): gain_rows[:, 0]]
where the time goes in v2:
time: 95.1 us; the launch traced here: 94.8 us
  Pallas kernels  90.3 us (95%)
  local copies, waits for them, and re-layouts  3.92 us (4%)
    pallas_call x1, Pallas kernels, body(): pl.pallas_call(layer_kernel, out_shape=[S(64, 12, 128), S(64, 12, 128), S...  89 us
    unnamed x10, local copies, waits for them, and re-layouts  3.92 us

profile of v2, /device:TPU:1, one launch (start us, length us, event | category | flops | bytes accessed | tf_op | source)
XLA Modules:
  0.0 94.8 jit_solution(15127245139226343373)
XLA Ops:
  0.6 0.0 copy-start.4
  0.6 89.0 %shard_map.92 = (f32[64,12,128]{2,1,0:T(8,128)}, f32[64,12,128]{2,1,0:T(8,128)}, f32[8,12,384]{2,1,0:T(8,128)}, f32[12,2304]{1,0:T(8,128)}) custom-call(f32[128,768]{1,0:T(8,128)} %bitcast.4, f32[128,768]{1,0:T(8,128)} %bitcast.5, f32[768]{0:T(1024)} %g_ref.3, f32[768,2304]{1,0:T(8,128)} %wq_hbm.1, f32[768,768]{1,0:T(8,128)} %wo_hbm.1), custom_call_target="tpu_custom_call" | custom-call | tf_op jit(solution)/shard_map/pallas_call | solution.py:435
  89.7 0.0 copy-done.4
  89.7 0.0 copy-start
  89.7 1.0 %copy-done = f32[64,12,128]{2,1,0:T(8,128)S(1)} copy-done((f32[64,12,128]{2,1,0:T(8,128)S(1)}, f32[64,12,128]{2,1,0:T(8,128)}, u32[]{:S(2)}) %copy-start) | copy-done | bytes 393240
  90.7 0.0 copy-start.1
  90.7 1.0 %copy-done.1 = f32[64,12,128]{2,1,0:T(8,128)S(1)} copy-done((f32[64,12,128]{2,1,0:T(8,128)S(1)}, f32[64,12,128]{2,1,0:T(8,128)}, u32[]{:S(2)}) %copy-start.1) | copy-done | bytes 393240
  91.8 0.0 copy-start.2
  91.8 0.9 copy-done.2
  92.7 0.0 copy-start.3
  92.7 0.9 copy-done.3
  93.6 1.2 %shard_map.93 = (f32[128,768]{1,0:T(8,128)}, f32[128,768]{1,0:T(8,128)}, f32[12,2304]{1,0:T(8,128)}, f32[12,768]{1,0:T(8,128)}, f32[12]{0:T(128)}) custom-call(f32[64,12,128]{2,1,0:T(8,128)S(1)} %copy-done, f32[64,12,128]{2,1,0:T(8,128)S(1)} %copy-done.1, f32[8,12,384]{2,1,0:T(8,128)S(1)} %copy-done.2, f32[12,2304]{1,0:T(8,128)S(1)} %copy-done.3, ...), custom_call_target="tpu_custom_call" | custom-call | tf_op jit(solution)/shard_map/pallas_call | solution.py:450
Async XLA Ops:
  0.6 89.0 %copy-start.4 = (f32[768]{0:T(1024)S(1)}, f32[768]{0:T(1024)}, u32[]{:S(2)}) copy-start(f32[768]{0:T(1024)} %g_ref.3) | copy-start | bytes 9220
  89.7 1.0 %copy-start = (f32[64,12,128]{2,1,0:T(8,128)S(1)}, f32[64,12,128]{2,1,0:T(8,128)}, u32[]{:S(2)}) copy-start(f32[64,12,128]{2,1,0:T(8,128)} %get-tuple-element.14.recv_o) | copy-start | bytes 1179652
  90.7 1.0 %copy-start.1 = (f32[64,12,128]{2,1,0:T(8,128)S(1)}, f32[64,12,128]{2,1,0:T(8,128)}, u32[]{:S(2)}) copy-start(f32[64,12,128]{2,1,0:T(8,128)} %get-tuple-element.15.recv_g) | copy-start | bytes 1179652
  91.8 0.9 copy-start.2
  92.7 0.9 copy-start.3

commit v3 on v2

--- a/solution.py
+++ b/solution.py
@@ -82,16 +82,20 @@
     for n in range(0, 768, 256):
         out[:, n:n + 256] = t[:, n:n + 256] + product(m_hi, m_lo, woh[:, n:n + 256], wol[:, n:n + 256])
 
-def backward_attn(u, woh, wol, qkv, probs, dmix, dqkv):
+def back_values(u, woh, wol, probs, dmix, dqkv):
     u_hi, u_lo = split(u)
     for n in range(0, 768, 256):
         dmix[:, n:n + 256] = product(u_hi, u_lo, woh[n:n + 256, :], wol[n:n + 256, :], 1)
     for p in range(6):
         c = 128 * p
-        do = dmix[:, c:c + 128]
+        dqkv[:, 1536 + c:1536 + c + 128] = back_heads(probs[:, 256 * p:256 * p + 256], dmix[:, c:c + 128])
+
+
+def back_scores(qkv, probs, dmix, dqkv):
+    for p in range(6):
+        c = 128 * p
         pr = probs[:, 256 * p:256 * p + 256]
-        dqkv[:, 1536 + c:1536 + c + 128] = back_heads(pr, do)
-        dp = by_heads(do, head_pair(qkv[:, 1536 + c:1536 + c + 128]))
+        dp = by_heads(dmix[:, c:c + 128], head_pair(qkv[:, 1536 + c:1536 + c + 128]))
         ds = []
         for h in range(2):
             a, b = pr[:, 128 * h:128 * h + 128], dp[:, 128 * h:128 * h + 128]
@@ -99,6 +103,7 @@
         ds = cols2(*ds)
         dqkv[:, c:c + 128] = 0.125 * mix_heads(ds, head_pair(qkv[:, 768 + c:768 + c + 128]))
         dqkv[:, 768 + c:768 + c + 128] = back_heads(ds, qkv[:, c:c + 128])
+
 
 def backward_norm(u, gain, wqh, wql, xhat_ref, inv_ref, dqkv, tg):
     d_hi, d_lo = split(dqkv[...])
@@ -182,56 +187,87 @@
     return {"a": (t ^ 1, q), "b": (t ^ 3, q), "c": (t, q ^ 2), "d": (t ^ 4, q ^ 2)}[dim]
 
 
-DIMS = "abcd"
-AXIS = {"a": 0, "c": 1, "d": 3, "b": 4}
-PARTS = (0, 1, 4, 5, 2, 3, 6, 7)
-
-
-def order(part):
-    return [DIMS[(part // 2 + s) % 4] for s in range(4)]
-
-
-def extents(part, step):
+AXIS = {"a": (0, 1), "c": (1, 0), "d": (3, None), "b": (4, None)}
+SUBS = ((0, 0, 256), (0, 256, 128), (1, 0, 256), (1, 256, 128))
+PLAN = (
+    'value',
+    0,
+    'scores',
+    1,
+    2,
+    (0, 0),
+    3,
+    'norm',
+    (1, 0),
+    (0, 1),
+    (2, 0),
+    (1, 1),
+    (0, 2),
+    (3, 0),
+    'return',
+    (2, 1),
+    (1, 2),
+    (0, 3),
+    (3, 1),
+    (2, 2),
+    (1, 3),
+    (3, 2),
+    (2, 3),
+    (3, 3),
+)
+
+
+def order(chunk, sub):
+    return ["abcd"[(chunk + sub + s) % 4] for s in range(4)]
+
+
+def extents(chunk, sub, step):
     size = [2, 2, 1, 2, 2]
-    for dim in order(part)[:step + 1]:
-        size[AXIS[dim]] = 1
+    for dim in order(chunk, sub)[:step + 1]:
+        size[AXIS[dim][0]] = 1
     return size
 
 
-def select(part, step, own, other):
-    at = [pl.ds(0, 2), pl.ds(0, 2), pl.ds(part, 1), pl.ds(0, 2), pl.ds(0, 2)]
-    for s, dim in enumerate(order(part)[:step + 1]):
-        bit = own[dim]
-        at[AXIS[dim]] = pl.ds(1 - bit if other and s == step else bit, 1)
-    return tuple(at)
-
-
-def reduce_copy(part, step, own, terms, landing, sems):
+def select(chunk, sub, step, own, other):
+    z0, col, cols = SUBS[sub]
+    at = [pl.ds(0, 2), pl.ds(0, 2), pl.ds(z0, 1), pl.ds(0, 2), pl.ds(0, 2)]
+    for s, dim in enumerate(order(chunk, sub)[:step + 1]):
+        axis, place_in = AXIS[dim]
+        bit = own[dim] if place_in is None else own[dim] ^ ((chunk >> place_in) & 1)
+        at[axis] = pl.ds(1 - bit if other and s == step else bit, 1)
+    return at
+
+
+def reduce_copy(chunk, sub, step, own, terms, landing, sems):
+    z0, col, cols = SUBS[sub]
     return pltpu.make_async_remote_copy(
-        terms.at[select(part, step, own, True)],
-        landing[step][part],
-        sems.at[0, step, part],
-        sems.at[1, step, part],
-        device_id=partner(order(part)[step]),
+        terms.at[(chunk, *select(chunk, sub, step, own, True), slice(None), pl.ds(col, cols))],
+        landing[step][4 * chunk + sub],
+        sems.at[0, step, 4 * chunk + sub],
+        sems.at[1, step, 4 * chunk + sub],
+        device_id=partner(order(chunk, sub)[step]),
         device_id_type=MESH,
     )
 
 
-def reduce_add(part, step, own, terms, landing):
-    at = select(part, step, own, False)
-    size = extents(part, step)
-    buf = landing[step][part]
-    for i in range(size[0]):
-        for j in range(size[1]):
-            for k in range(size[2]):
-                for m in range(size[3]):
-                    for n in range(size[4]):
-                        idx = tuple(s.start + o for s, o in zip(at, (i, j, k, m, n)))
-                        terms[idx] = terms[idx] + buf[i, j, k, m, n]
+def reduce_add(chunk, sub, step, own, terms, landing):
+    z0, col, cols = SUBS[sub]
+    at = select(chunk, sub, step, own, False)
+    size = extents(chunk, sub, step)
+    buf = landing[step][4 * chunk + sub]
+    for n in range(size[0] * size[1] * size[3] * size[4]):
+        pos, left = [0] * 5, n
+        for axis in (4, 3, 1, 0):
+            pos[axis], left = left % size[axis], left // size[axis]
+        idx = (chunk, *(s.start + o for s, o in zip(at, pos)), slice(None), slice(col, col + cols))
+        terms[idx] = terms[idx] + buf[tuple(pos)]
 
 
 def landing_shapes():
-    return [pltpu.VMEM(tuple(extents(part, step)) + (24, 384), F32) for step in range(4) for part in range(8)]
+    return [
+        pltpu.VMEM(tuple(extents(k, s, step)) + (24, SUBS[s][2]), F32)
+        for step in range(4) for k in range(4) for s in range(4)
+    ]
 
 
 def group_peers():
@@ -264,11 +300,11 @@
     tok, wq, wo, wrows, up,
     wqh, wql, woh, wol, t_ref, u_ref, out, tg, xhat, inv, qkv, probs, mix, dmix, dqkv,
     send_t, send_u, send_o, send_g, recv_t, recv_u, recv_o, recv_g,
-    s_xhat, s_mix, s_dqkv, s_up, left, right, terms, recv_z, own_piece, pieces,
+    s_xhat, s_mix, s_u, s_v, s_k, s_q, left, right, terms, recv_z, own_piece, pieces,
     *rest,
 ):
-    landing = [rest[8 * s:8 * s + 8] for s in range(4)]
-    sem_in, sem_t, sem_u, sem_o, sem_g, sem_sib, sem_red, sem_z, sem_p, sem_out = rest[32:]
+    landing = [rest[16 * s:16 * s + 16] for s in range(4)]
+    sem_in, sem_t, sem_u, sem_o, sem_g, sem_sib, sem_red, sem_z, sem_p, sem_out = rest[64:]
     t, q = place()
     z, core = t // 8, lax.rem(q, 2)
     own = bits()
@@ -278,8 +314,8 @@
         pltpu.make_async_copy(src, dst, sem_in.at[k])
         for k, (src, dst) in enumerate(((tok_hbm, tok), (up_hbm, up), (wq_hbm, wq), (wo_hbm, wo)))
     ]
-    for load in loads:
-        load.start()
+    loads[0].start()
+    loads[1].start()
     greet(extra)
     loads[0].wait()
     pack(tok, send_t)
@@ -288,6 +324,8 @@
     loads[1].wait()
     pack(up, send_u)
     exchange_start(send_u, recv_u, sem_u)
+    loads[2].start()
+    loads[3].start()
     loads[2].wait()
     prep_weights(wq, wqh, wql, 256)
     own_rows(wq, wrows)
@@ -314,56 +352,71 @@
         join_left(left, k, a[...], b[...])
     exchange_wait(send_u, recv_u, sem_u)
     unpack(recv_u, into(u_ref))
-    sib_u = sibling_copy(u_ref.at[:, pl.ds(pl.multiple_of((1 - core) * 384, 128), 384)], s_up, sem_sib, 2)
-    sib_u.start()
-    backward_attn(u_ref[...], woh, wol, qkv, probs, dmix, dqkv)
-    sib_d = sibling_copy(dqkv.at[:, pl.ds(pl.multiple_of((1 - core) * 1152, 128), 1152)], s_dqkv, sem_sib, 3)
-    sib_d.start()
-    backward_norm(u_ref[...], gain, wqh, wql, xhat, inv, dqkv, tg)
-    sib_u.wait()
-    join_right(right, 3, u_ref[:, pl.ds(pl.multiple_of(core * 384, 128), 384)], s_up[...])
-    sib_d.wait()
-    for j in range(3):
-        col = pl.ds(pl.multiple_of(core * 1152 + 384 * j, 128), 384)
-        join_right(right, j, dqkv[:, col], s_dqkv[:, 384 * j:384 * j + 384])
-
-    def block(r, i, j):
-        g = 2 * i + j
-        v = dot(left[g // 3, 192 * r:192 * r + 192, :], right[g])
-        terms[i, j, 2 * r:2 * r + 2] = v.reshape(2, 2, 2, 24, 384)
-
-    def begin(p, step):
-        reduce_copy(p, step, own, terms, landing, sem_red).start()
+
+    def half(ref, start, k):
+        return ref.at[:, pl.ds(pl.multiple_of(start + k * 384, 128), 384)]
+
+    sources = ((u_ref, 0, s_u), (dqkv, 1536, s_v), (dqkv, 768, s_k), (dqkv, 0, s_q))
+
+    def share(k):
+        ref, start, landed = sources[k]
+        return sibling_copy(half(ref, start, 1 - core), landed, sem_sib, 2 + k)
+
+    def chunk(k):
+        share(k).wait()
+        ref, start, landed = sources[k]
+        join_right(right, k, half(ref, start, core)[...], landed[...])
+        for r in range(4):
+            v = dot(left[1 if k == 0 else 0, 192 * r:192 * r + 192, :], right[k])
+            terms[k, r // 2, r % 2] = v.reshape(2, 2, 2, 24, 384)
+        for s in range(4):
+            reduce_copy(k, s, 0, own, terms, landing, sem_red).start()
 
     a, c = own["a"], own["c"]
-    both = (0, 1)
-    for r, blocks in ((0, [(1 - a, j) for j in both]), (2, [(i, 1 - c) for i in both]), (1, None), (3, None)):
-        for i, j in blocks or [(i, j) for i in both for j in both]:
-            block(r, i, j)
-        begin(2 * r, 0)
-        begin(2 * r + 1, 0)
-    for j in both:
-        block(0, a, j)
-    for i in both:
-        block(2, i, c)
-    pack(tg, send_g)
-    exchange_start(send_g, recv_g, sem_g)
-    for step in range(4):
-        for p in PARTS:
-            reduce_copy(p, step, own, terms, landing, sem_red).wait()
-            reduce_add(p, step, own, terms, landing)
+
+    def arrive(k, step):
+        for s in range(4):
+            reduce_copy(k, s, step, own, terms, landing, sem_red).wait()
+            reduce_add(k, s, step, own, terms, landing)
             if step < 3:
-                begin(p, step + 1)
-            else:
-
-                @pl.when(z != p)
-                def _(p=p):
-                    pltpu.make_async_remote_copy(
-                        terms.at[a, c, p, own["d"], own["b"]], recv_z.at[z], sem_z.at[0], sem_z.at[1],
-                        device_id=(p * 8 + lax.rem(t, 8), q), device_id_type=MESH,
-                    ).start()
-
-    recv_z[pl.ds(z, 1)] = terms[a, c, pl.ds(z, 1), own["d"], own["b"]]
+                reduce_copy(k, s, step + 1, own, terms, landing, sem_red).start()
+        if step < 3:
+            return
+        z2, z1 = a ^ (k >> 1), c ^ (k & 1)
+        for z0 in range(2):
+            to = 4 * z2 + 2 * z1 + z0
+            block = terms.at[k, z2, z1, z0, own["d"], own["b"]]
+
+            @pl.when(z != to)
+            def _(to=to, block=block):
+                pltpu.make_async_remote_copy(
+                    block, recv_z.at[z], sem_z.at[0], sem_z.at[1],
+                    device_id=(to * 8 + lax.rem(t, 8), q), device_id_type=MESH,
+                ).start()
+
+            @pl.when(z == to)
+            def _(block=block):
+                recv_z[pl.ds(z, 1)] = block[...].reshape(1, 24, 384)
+
+    share(0).start()
+    for task in PLAN:
+        if task == "value":
+            back_values(u_ref[...], woh, wol, probs, dmix, dqkv)
+            share(1).start()
+        elif task == "scores":
+            back_scores(qkv, probs, dmix, dqkv)
+            share(2).start()
+            share(3).start()
+        elif task == "norm":
+            backward_norm(u_ref[...], gain, wqh, wql, xhat, inv, dqkv, tg)
+        elif task == "return":
+            pack(tg, send_g)
+            exchange_start(send_g, recv_g, sem_g)
+        elif isinstance(task, int):
+            chunk(task)
+        else:
+            arrive(*task)
+
     exchange_wait(send_o, recv_o, sem_o)
     exchange_wait(send_g, recv_g, sem_g)
     results = [
@@ -382,7 +435,7 @@
         total = total + recv_z[k]
     own_piece[0] = total[:12]
     own_piece[1] = total[12:]
-    me = core * 4 + a * 2 + c
+    me = core * 4 + (a ^ (z // 4)) * 2 + (c ^ lax.rem(z // 2, 2))
     copies = []
     for k, (pt, pq) in enumerate(peers):
         copy = pltpu.make_async_remote_copy(
@@ -405,10 +458,10 @@
     gain = jnp.sum(jnp.where(lane == row + 12 * t, g_ref[...].reshape(1, 768), 0.0), axis=1, keepdims=True)
     gain_sum = jnp.zeros((12, 1), F32)
     for k in range(8):
-        j, c = k % 4, k // 4
+        chunk, c = k % 4, k // 4
         piece = pieces[k]
-        if j < 3:
-            col = 1152 * c + 384 * j
+        if chunk:
+            col = 768 * (3 - chunk) + 384 * c
             qkv_rows[:, col:col + 384] = piece * gain
             gain_sum = gain_sum + jnp.sum(piece * wrows[:, col:col + 384], axis=1, keepdims=True)
         else:
@@ -441,10 +494,10 @@
         + [H(768, 2304), H(768, 2304), H(768, 768), H(768, 768)]
         + [rows, rows, rows, rows, rows, V(128, 128), V(128, 2304), V(128, 1536), rows, rows, V(128, 2304)]
         + [pack_buffer] * 8
-        + [rows, rows, V(128, 1152), V(128, 384), H(2, 768, 768), H(4, 768, 384)]
-        + [V(2, 2, 8, 2, 2, 24, 384), V(8, 24, 384), V(2, 12, 384), V(8, 12, 384)]
+        + [rows, rows, V(128, 384), V(128, 384), V(128, 384), V(128, 384), H(2, 768, 768), H(4, 768, 384)]
+        + [V(4, 2, 2, 2, 2, 2, 24, 384), V(8, 24, 384), V(2, 12, 384), V(8, 12, 384)]
         + landing_shapes()
-        + [D(4), D(2), D(2), D(2), D(2), D(2, 4), D(2, 4, 8), D(2), D(2, 7), D(4)],
+        + [D(4), D(2), D(2), D(2), D(2), D(2, 6), D(2, 4, 16), D(2), D(2, 7), D(4)],
         compiler_params=pltpu.CompilerParams(collective_id=0, has_side_effects=True, vmem_limit_bytes=60 * 2 ** 20),
     )(tok, up, norm_gain_vector, qkv_weight, out_weight)
     out, tg, qkv_rows, out_rows, gain_rows = pl.pallas_call(
@@ -452,7 +505,7 @@
         out_shape=[S(128, 768), S(128, 768), S(12, 2304), S(12, 768), S(12)],
         in_specs=[vmem] * 5,
         out_specs=[vmem] * 5,
-        compiler_params=pltpu.CompilerParams(vmem_limit_bytes=16 * 2 ** 20),
+        compiler_params=pltpu.CompilerParams(vmem_limit_bytes=60 * 2 ** 20),
     )(recv_o, recv_g, pieces, wrows, norm_gain_vector)
     return out.reshape(shape), tg.reshape(shape), qkv_rows, out_rows, gain_rows
 

time: 95.1 us -> 89 us (0.936)
  local copies, waits for them, and re-layouts: 3.92 us -> 0 us
  Pallas kernels: 90.3 us -> 88.2 us
    unnamed x10 -> x0, local copies, waits for them, and re-layouts: 3.92 us -> none
    pallas_call x1, Pallas kernels: 89 us -> 85.6 us  [body(): pl.pallas_call(layer_kernel, out_shape=[S(64, 12, 128), S(64, 12, 128), S...]
    pallas_call x1, Pallas kernels: 1.23 us -> 2.52 us  [body(): pl.pallas_call(finish_kernel, out_shape=[S(128, 768), S(128, 768), S(12,...]
where the time goes in v3:
time: 89 us; the launch traced here: 88.8 us
  Pallas kernels  88.2 us (99%)
    pallas_call x1, Pallas kernels, body(): pl.pallas_call(layer_kernel, out_shape=[S(64, 12, 128), S(64, 12, 128), S...  85.6 us
    pallas_call x1, Pallas kernels, body(): pl.pallas_call(finish_kernel, out_shape=[S(128, 768), S(128, 768), S(12,...  2.52 us

profile of v3, /device:TPU:1, one launch (start us, length us, event | category | flops | bytes accessed | tf_op | source)
XLA Modules:
  0.0 88.8 jit_solution(155454627269726240)
XLA Ops:
  0.6 85.6 %shard_map.92 = (f32[64,12,128]{2,1,0:T(8,128)}, f32[64,12,128]{2,1,0:T(8,128)}, f32[8,12,384]{2,1,0:T(8,128)}, f32[12,2304]{1,0:T(8,128)}) custom-call(f32[128,768]{1,0:T(8,128)} %bitcast.4, f32[128,768]{1,0:T(8,128)} %bitcast.5, f32[768]{0:T(1024)} %g_ref.3, f32[768,2304]{1,0:T(8,128)} %wq_hbm.1, f32[768,768]{1,0:T(8,128)} %wo_hbm.1), custom_call_target="tpu_custom_call" | custom-call | tf_op jit(solution)/shard_map/pallas_call | solution.py:488
  86.3 2.5 %shard_map.93 = (f32[128,768]{1,0:T(8,128)}, f32[128,768]{1,0:T(8,128)}, f32[12,2304]{1,0:T(8,128)}, f32[12,768]{1,0:T(8,128)}, f32[12]{0:T(128)}) custom-call(f32[64,12,128]{2,1,0:T(8,128)} %get-tuple-element.14.recv_o, f32[64,12,128]{2,1,0:T(8,128)} %get-tuple-element.15.recv_g, f32[8,12,384]{2,1,0:T(8,128)} %get-tuple-element.16.pieces, ...), custom_call_target="tpu_custom_call" | custom-call | tf_op jit(solution)/shard_map/pallas_call | solution.py:503

commit v4 on v3

--- a/solution.py
+++ b/solution.py
@@ -119,6 +119,17 @@
     return lax.axis_index("tm"), lax.axis_index("patch")
 
 
+def far_first():
+    steps = [(dz, dy, dx) for dz in range(8) for dy in range(2) for dx in range(4)][1:]
+    return sorted(steps, key=lambda v: -(min(v[0], 8 - v[0]) + 2 * v[1] + min(v[2], 4 - v[2])))
+
+
+def others():
+    t, _ = place()
+    z, y, x = t // 8, lax.rem(t // 4, 2), lax.rem(t, 4)
+    return [(lax.rem(z + dz, 8) * 2 + (y ^ dy)) * 4 + lax.rem(x + dx, 4) for dz, dy, dx in far_first()]
+
+
 def pack(value, send):
     for i in range(2):
         for c in range(6):
@@ -135,9 +146,8 @@
     t, q = place()
     barrier = pltpu.get_barrier_semaphore()
 
-    @pl.loop(1, 64)
-    def _(k):
-        pl.semaphore_signal(barrier, inc=1, device_id=(t ^ k, q), device_id_type=MESH)
+    for peer in others():
+        pl.semaphore_signal(barrier, inc=1, device_id=(peer, q), device_id_type=MESH)
 
     for peer in extra:
         pl.semaphore_signal(barrier, inc=1, device_id=peer, device_id_type=MESH)
@@ -150,9 +160,7 @@
 def exchange_start(send, received, sems):
     t, q = place()
 
-    @pl.loop(1, 64)
-    def _(k):
-        peer = lax.rem(t + k, 64)
+    for peer in others():
         pltpu.make_async_remote_copy(
             send.at[peer], received.at[t], sems.at[0], sems.at[1], device_id=(peer, q), device_id_type=MESH
         ).start()
@@ -178,17 +186,25 @@
 
 def bits():
     t, q = place()
-    x, yh, yl = lax.rem(t, 4), lax.rem(t // 4, 2), q // 2
-    return {"a": lax.rem(x, 2) ^ (x // 2), "b": x // 2, "c": yl ^ yh, "d": yh}
+    x, yh, yl, z0 = lax.rem(t, 4), lax.rem(t // 4, 2), q // 2, lax.rem(t // 8, 2)
+    return {"a": lax.rem(x, 2) ^ (x // 2), "b": x // 2, "c": yl ^ yh, "d": yh, "e": z0, "f": z0}
 
 
 def partner(dim):
     t, q = place()
-    return {"a": (t ^ 1, q), "b": (t ^ 3, q), "c": (t, q ^ 2), "d": (t ^ 4, q ^ 2)}[dim]
-
-
-AXIS = {"a": (0, 1), "c": (1, 0), "d": (3, None), "b": (4, None)}
-SUBS = ((0, 0, 256), (0, 256, 128), (1, 0, 256), (1, 256, 128))
+    if dim == "f":
+        return (lax.rem(t + jnp.where(lax.rem(t // 8, 2) == 0, 56, 8), 64), q)
+    return {"a": (t ^ 1, q), "b": (t ^ 3, q), "c": (t, q ^ 2), "d": (t ^ 4, q ^ 2), "e": (t ^ 8, q)}[dim]
+
+
+AXIS = {"a": (0, 1), "c": (1, 0), "d": (3, None), "b": (4, None), "e": (2, None), "f": (2, None)}
+SUBS = (
+    ((None, 0, 128, "eabcd"), (None, 128, 128, "fbcda"), (0, 256, 128, "cdab"), (1, 256, 128, "dabc")),
+    ((None, 0, 128, "ecdab"), (None, 128, 128, "fdabc"), (0, 256, 128, "abcd"), (1, 256, 128, "bcda")),
+    ((0, 0, 256, "cdab"), (0, 256, 128, "dabc"), (1, 0, 256, "abcd"), (1, 256, 128, "bcda")),
+    ((0, 0, 256, "dabc"), (0, 256, 128, "abcd"), (1, 0, 256, "bcda"), (1, 256, 128, "cdab")),
+)
+BY_Z = (0, 1)
 PLAN = (
     'value',
     0,
@@ -196,7 +212,6 @@
     1,
     2,
     (0, 0),
-    3,
     'norm',
     (1, 0),
     (0, 1),
@@ -204,33 +219,35 @@
     (1, 1),
     (0, 2),
     (3, 0),
-    'return',
     (2, 1),
     (1, 2),
+    'return',
     (0, 3),
     (3, 1),
     (2, 2),
     (1, 3),
+    (0, 4),
     (3, 2),
+    (1, 4),
     (2, 3),
     (3, 3),
 )
 
 
 def order(chunk, sub):
-    return ["abcd"[(chunk + sub + s) % 4] for s in range(4)]
+    return SUBS[chunk][sub][3]
 
 
 def extents(chunk, sub, step):
-    size = [2, 2, 1, 2, 2]
+    size = [2, 2, 2 if SUBS[chunk][sub][0] is None else 1, 2, 2]
     for dim in order(chunk, sub)[:step + 1]:
         size[AXIS[dim][0]] = 1
     return size
 
 
 def select(chunk, sub, step, own, other):
-    z0, col, cols = SUBS[sub]
-    at = [pl.ds(0, 2), pl.ds(0, 2), pl.ds(z0, 1), pl.ds(0, 2), pl.ds(0, 2)]
+    z0 = SUBS[chunk][sub][0]
+    at = [pl.ds(0, 2), pl.ds(0, 2), pl.ds(0, 2) if z0 is None else pl.ds(z0, 1), pl.ds(0, 2), pl.ds(0, 2)]
     for s, dim in enumerate(order(chunk, sub)[:step + 1]):
         axis, place_in = AXIS[dim]
         bit = own[dim] if place_in is None else own[dim] ^ ((chunk >> place_in) & 1)
@@ -239,35 +256,36 @@
 
 
 def reduce_copy(chunk, sub, step, own, terms, landing, sems):
-    z0, col, cols = SUBS[sub]
+    _, col, cols, dims = SUBS[chunk][sub]
     return pltpu.make_async_remote_copy(
         terms.at[(chunk, *select(chunk, sub, step, own, True), slice(None), pl.ds(col, cols))],
-        landing[step][4 * chunk + sub],
+        landing[chunk, sub, step],
         sems.at[0, step, 4 * chunk + sub],
         sems.at[1, step, 4 * chunk + sub],
-        device_id=partner(order(chunk, sub)[step]),
+        device_id=partner(dims[step]),
         device_id_type=MESH,
     )
 
 
 def reduce_add(chunk, sub, step, own, terms, landing):
-    z0, col, cols = SUBS[sub]
+    _, col, cols, _ = SUBS[chunk][sub]
     at = select(chunk, sub, step, own, False)
     size = extents(chunk, sub, step)
-    buf = landing[step][4 * chunk + sub]
-    for n in range(size[0] * size[1] * size[3] * size[4]):
+    buf = landing[chunk, sub, step]
+    for n in range(size[0] * size[1] * size[2] * size[3] * size[4]):
         pos, left = [0] * 5, n
-        for axis in (4, 3, 1, 0):
+        for axis in (4, 3, 2, 1, 0):
             pos[axis], left = left % size[axis], left // size[axis]
         idx = (chunk, *(s.start + o for s, o in zip(at, pos)), slice(None), slice(col, col + cols))
         terms[idx] = terms[idx] + buf[tuple(pos)]
 
 
+def landings():
+    return [(k, s, step) for k in range(4) for s in range(4) for step in range(len(order(k, s)))]
+
+
 def landing_shapes():
-    return [
-        pltpu.VMEM(tuple(extents(k, s, step)) + (24, SUBS[s][2]), F32)
-        for step in range(4) for k in range(4) for s in range(4)
-    ]
+    return [pltpu.VMEM(tuple(extents(*key)) + (24, SUBS[key[0]][key[1]][2]), F32) for key in landings()]
 
 
 def group_peers():
@@ -303,8 +321,8 @@
     s_xhat, s_mix, s_u, s_v, s_k, s_q, left, right, terms, recv_z, own_piece, pieces,
     *rest,
 ):
-    landing = [rest[16 * s:16 * s + 16] for s in range(4)]
-    sem_in, sem_t, sem_u, sem_o, sem_g, sem_sib, sem_red, sem_z, sem_p, sem_out = rest[64:]
+    landing = dict(zip(landings(), rest))
+    sem_in, sem_t, sem_u, sem_o, sem_g, sem_sib, sem_red, sem_z, sem_p, sem_out = rest[len(landing):]
     t, q = place()
     z, core = t // 8, lax.rem(q, 2)
     own = bits()
@@ -316,6 +334,7 @@
     ]
     loads[0].start()
     loads[1].start()
+    recv_z[...] = jnp.zeros_like(recv_z)
     greet(extra)
     loads[0].wait()
     pack(tok, send_t)
@@ -362,37 +381,52 @@
         ref, start, landed = sources[k]
         return sibling_copy(half(ref, start, 1 - core), landed, sem_sib, 2 + k)
 
-    def chunk(k):
-        share(k).wait()
-        ref, start, landed = sources[k]
-        join_right(right, k, half(ref, start, core)[...], landed[...])
+    def chunk(*ks):
+        for k in ks:
+            share(k).wait()
+            ref, start, landed = sources[k]
+            join_right(right, k, half(ref, start, core)[...], landed[...])
         for r in range(4):
-            v = dot(left[1 if k == 0 else 0, 192 * r:192 * r + 192, :], right[k])
-            terms[k, r // 2, r % 2] = v.reshape(2, 2, 2, 24, 384)
-        for s in range(4):
-            reduce_copy(k, s, 0, own, terms, landing, sem_red).start()
+            rows = left[1 if ks[0] == 0 else 0, 192 * r:192 * r + 192, :]
+            both = dot(rows, jnp.concatenate([right[k] for k in ks], 1))
+            for n, k in enumerate(ks):
+                terms[k, r // 2, r % 2] = both[:, 384 * n:384 * n + 384].reshape(2, 2, 2, 24, 384)
+        for k in ks:
+            for s in range(4):
+                reduce_copy(k, s, 0, own, terms, landing, sem_red).start()
 
     a, c = own["a"], own["c"]
 
     def arrive(k, step):
         for s in range(4):
+            steps = len(order(k, s))
+            if step >= steps:
+                continue
             reduce_copy(k, s, step, own, terms, landing, sem_red).wait()
             reduce_add(k, s, step, own, terms, landing)
-            if step < 3:
+            if step < steps - 1:
                 reduce_copy(k, s, step + 1, own, terms, landing, sem_red).start()
-        if step < 3:
+        if step < max(len(order(k, s)) for s in range(4)) - 1:
             return
         z2, z1 = a ^ (k >> 1), c ^ (k & 1)
         for z0 in range(2):
             to = 4 * z2 + 2 * z1 + z0
             block = terms.at[k, z2, z1, z0, own["d"], own["b"]]
-
-            @pl.when(z != to)
-            def _(to=to, block=block):
-                pltpu.make_async_remote_copy(
-                    block, recv_z.at[z], sem_z.at[0], sem_z.at[1],
-                    device_id=(to * 8 + lax.rem(t, 8), q), device_id_type=MESH,
-                ).start()
+            far = {"device_id": (to * 8 + lax.rem(t, 8), q), "device_id_type": MESH}
+
+            @pl.when((z != to) & (own["e"] == z0))
+            def _(block=block, far=far):
+                pltpu.make_async_remote_copy(block, recv_z.at[z], sem_z.at[0], sem_z.at[3], **far).start()
+
+            @pl.when(own["e"] != z0)
+            def _(block=block, far=far):
+                if k in BY_Z:
+                    last = pl.ds(256, 128)
+                    pltpu.make_async_remote_copy(
+                        block.at[:, last], recv_z.at[z, :, last], sem_z.at[1], sem_z.at[4], **far
+                    ).start()
+                else:
+                    pltpu.make_async_remote_copy(block, recv_z.at[z], sem_z.at[2], sem_z.at[4], **far).start()
 
             @pl.when(z == to)
             def _(block=block):
@@ -413,7 +447,7 @@
             pack(tg, send_g)
             exchange_start(send_g, recv_g, sem_g)
         elif isinstance(task, int):
-            chunk(task)
+            chunk(*((2, 3) if task == 2 else (task,)))
         else:
             arrive(*task)
 
@@ -425,17 +459,31 @@
     ]
     for result in results[:3]:
         result.start()
-    every = pltpu.make_async_remote_copy(
-        recv_z.at[pl.ds(0, 7)], recv_z.at[pl.ds(0, 7)], sem_z.at[0], sem_z.at[1], device_id=(t ^ 8, q), device_id_type=MESH
-    )
-    every.wait_send()
-    every.wait_recv()
+    held = (a ^ (z // 4)) * 2 + (c ^ lax.rem(z // 2, 2))
+
+    def landed(n, cols, k):
+        ref = recv_z.at[pl.ds(0, n), :, pl.ds(0, cols)]
+        return pltpu.make_async_copy(ref, ref, sem_z.at[k])
+
+    landed(3, 384, 0).wait()
+    landed(2, 128, 1).wait()
+    landed(2, 384, 2).wait()
+    landed(3, 384, 3).wait()
+
+    @pl.when(held < 2)
+    def _():
+        landed(4, 128, 4).wait()
+
+    @pl.when(held >= 2)
+    def _():
+        landed(4, 384, 4).wait()
+
     total = recv_z[0]
     for k in range(1, 8):
         total = total + recv_z[k]
     own_piece[0] = total[:12]
     own_piece[1] = total[12:]
-    me = core * 4 + (a ^ (z // 4)) * 2 + (c ^ lax.rem(z // 2, 2))
+    me = core * 4 + held
     copies = []
     for k, (pt, pq) in enumerate(peers):
         copy = pltpu.make_async_remote_copy(
@@ -497,7 +545,7 @@
         + [rows, rows, V(128, 384), V(128, 384), V(128, 384), V(128, 384), H(2, 768, 768), H(4, 768, 384)]
         + [V(4, 2, 2, 2, 2, 2, 24, 384), V(8, 24, 384), V(2, 12, 384), V(8, 12, 384)]
         + landing_shapes()
-        + [D(4), D(2), D(2), D(2), D(2), D(2, 6), D(2, 4, 16), D(2), D(2, 7), D(4)],
+        + [D(4), D(2), D(2), D(2), D(2), D(2, 6), D(2, 5, 16), D(5), D(2, 7), D(4)],
         compiler_params=pltpu.CompilerParams(collective_id=0, has_side_effects=True, vmem_limit_bytes=60 * 2 ** 20),
     )(tok, up, norm_gain_vector, qkv_weight, out_weight)
     out, tg, qkv_rows, out_rows, gain_rows = pl.pallas_call(

time: 89 us -> 84.9 us (0.954)
  Pallas kernels: 88.2 us -> 84.1 us
    pallas_call x1, Pallas kernels: 85.6 us -> 81.6 us  [body(): pl.pallas_call(layer_kernel, out_shape=[S(64, 12, 128), S(64, 12, 128), S...]
where the time goes in v4:
time: 84.9 us; the launch traced here: 84.8 us
  Pallas kernels  84.1 us (99%)
    pallas_call x1, Pallas kernels, body(): pl.pallas_call(layer_kernel, out_shape=[S(64, 12, 128), S(64, 12, 128), S...  81.6 us
    pallas_call x1, Pallas kernels, body(): pl.pallas_call(finish_kernel, out_shape=[S(128, 768), S(128, 768), S(12,...  2.52 us

profile of v4, /device:TPU:1, one launch (start us, length us, event | category | flops | bytes accessed | tf_op | source)
XLA Modules:
  0.0 84.8 jit_solution(6305234830608873522)
XLA Ops:
  0.6 81.6 %shard_map.92 = (f32[64,12,128]{2,1,0:T(8,128)}, f32[64,12,128]{2,1,0:T(8,128)}, f32[8,12,384]{2,1,0:T(8,128)}, f32[12,2304]{1,0:T(8,128)}) custom-call(f32[128,768]{1,0:T(8,128)} %bitcast.4, f32[128,768]{1,0:T(8,128)} %bitcast.5, f32[768]{0:T(1024)} %g_ref.3, f32[768,2304]{1,0:T(8,128)} %wq_hbm.1, f32[768,768]{1,0:T(8,128)} %wo_hbm.1), custom_call_target="tpu_custom_call" | custom-call | tf_op jit(solution)/shard_map/pallas_call | solution.py:536
  82.2 2.5 %shard_map.93 = (f32[128,768]{1,0:T(8,128)}, f32[128,768]{1,0:T(8,128)}, f32[12,2304]{1,0:T(8,128)}, f32[12,768]{1,0:T(8,128)}, f32[12]{0:T(128)}) custom-call(f32[64,12,128]{2,1,0:T(8,128)} %get-tuple-element.14.recv_o, f32[64,12,128]{2,1,0:T(8,128)} %get-tuple-element.15.recv_g, f32[8,12,384]{2,1,0:T(8,128)} %get-tuple-element.16.pieces, ...), custom_call_target="tpu_custom_call" | custom-call | tf_op jit(solution)/shard_map/pallas_call | solution.py:551

commit v5 on v4

--- a/solution.py
+++ b/solution.py
@@ -212,8 +212,8 @@
     1,
     2,
     (0, 0),
+    (1, 0),
     'norm',
-    (1, 0),
     (0, 1),
     (2, 0),
     (1, 1),
@@ -222,6 +222,7 @@
     (2, 1),
     (1, 2),
     'return',
+    'take',
     (0, 3),
     (3, 1),
     (2, 2),
@@ -290,7 +291,7 @@
 
 def group_peers():
     t, q = place()
-    return [(t ^ dx, q ^ dq) for dx in (0, 1) for dq in range(4) if dx or dq]
+    return [(t ^ dx, q ^ dq) for dx in (1, 0) for dq in (3, 2, 1, 0) if dx or dq]
 
 
 def sibling_copy(src, dst, sems, k):
@@ -327,7 +328,7 @@
     z, core = t // 8, lax.rem(q, 2)
     own = bits()
     peers = group_peers()
-    extra = [p for k, p in enumerate(peers) if k != 3] + [(t ^ 4, q ^ 2)]
+    extra = [(pt, pq) for pt, pq in peers[:3] + peers[4:]] + [(t ^ 4, q ^ 2)]
     loads = [
         pltpu.make_async_copy(src, dst, sem_in.at[k])
         for k, (src, dst) in enumerate(((tok_hbm, tok), (up_hbm, up), (wq_hbm, wq), (wo_hbm, wo)))
@@ -398,7 +399,7 @@
     a, c = own["a"], own["c"]
 
     def arrive(k, step):
-        for s in range(4):
+        for s in (range(4) if k in BY_Z else (1, 3, 0, 2)):
             steps = len(order(k, s))
             if step >= steps:
                 continue
@@ -432,6 +433,10 @@
             def _(block=block):
                 recv_z[pl.ds(z, 1)] = block[...].reshape(1, 24, 384)
 
+    results = [
+        pltpu.make_async_copy(src, dst, sem_out.at[k])
+        for k, (src, dst) in enumerate(((out, o_hbm), (tg, g_hbm), (wrows, w_hbm), (pieces, p_hbm)))
+    ]
     share(0).start()
     for task in PLAN:
         if task == "value":
@@ -443,6 +448,11 @@
             share(3).start()
         elif task == "norm":
             backward_norm(u_ref[...], gain, wqh, wql, xhat, inv, dqkv, tg)
+        elif task == "take":
+            exchange_wait(send_o, recv_o, sem_o)
+            unpack(recv_o, into(out))
+            results[0].start()
+            results[2].start()
         elif task == "return":
             pack(tg, send_g)
             exchange_start(send_g, recv_g, sem_g)
@@ -451,14 +461,9 @@
         else:
             arrive(*task)
 
-    exchange_wait(send_o, recv_o, sem_o)
     exchange_wait(send_g, recv_g, sem_g)
-    results = [
-        pltpu.make_async_copy(src, dst, sem_out.at[k])
-        for k, (src, dst) in enumerate(((recv_o, o_hbm), (recv_g, g_hbm), (wrows, w_hbm), (pieces, p_hbm)))
-    ]
-    for result in results[:3]:
-        result.start()
+    unpack(recv_g, into(tg))
+    results[1].start()
     held = (a ^ (z // 4)) * 2 + (c ^ lax.rem(z // 2, 2))
 
     def landed(n, cols, k):
@@ -499,11 +504,22 @@
         result.wait()
 
 
-def finish_kernel(recv_o, recv_g, pieces, wrows, g_ref, out, tg, qkv_rows, out_rows, gain_rows):
+def finish_kernel(
+    o_hbm, g_hbm, p_hbm, w_hbm, gain_hbm, out, tg, qkv_out, out_out, gain_out,
+    o_ref, g_ref, pieces, wrows, gain_ref, qkv_rows, out_rows, gain_rows, sems,
+):
     t, _ = place()
+    pairs = ((p_hbm, pieces), (w_hbm, wrows), (gain_hbm, gain_ref), (o_hbm, o_ref), (g_hbm, g_ref))
+    loads = [pltpu.make_async_copy(src, dst, sems.at[k]) for k, (src, dst) in enumerate(pairs)]
+    pairs = ((qkv_rows, qkv_out), (out_rows, out_out), (gain_rows, gain_out), (o_ref, out), (g_ref, tg))
+    stores = [pltpu.make_async_copy(src, dst, sems.at[5 + k]) for k, (src, dst) in enumerate(pairs)]
+    for load in loads:
+        load.start()
+    for load in loads[:3]:
+        load.wait()
     lane = lax.broadcasted_iota(jnp.int32, (12, 768), 1)
     row = lax.broadcasted_iota(jnp.int32, (12, 768), 0)
-    gain = jnp.sum(jnp.where(lane == row + 12 * t, g_ref[...].reshape(1, 768), 0.0), axis=1, keepdims=True)
+    gain = jnp.sum(jnp.where(lane == row + 12 * t, gain_ref[...].reshape(1, 768), 0.0), axis=1, keepdims=True)
     gain_sum = jnp.zeros((12, 1), F32)
     for k in range(8):
         chunk, c = k % 4, k // 4
@@ -515,12 +531,13 @@
         else:
             out_rows[:, 384 * c:384 * c + 384] = piece
     gain_rows[...] = gain_sum.reshape(12)
-    for recv, o in ((recv_o, out), (recv_g, tg)):
-
-        def store(i, c, v, o=o):
-            o[64 * i:64 * i + 64, 128 * c:128 * c + 128] = v
-
-        unpack(recv, store)
+    for store in stores[:3]:
+        store.start()
+    for load, store in zip(loads[3:], stores[3:]):
+        load.wait()
+        store.start()
+    for store in stores:
+        store.wait()
 
 
 def body(tokens, norm_gain_vector, qkv_weight, out_weight, upstream):
@@ -533,9 +550,9 @@
     D = lambda *s: pltpu.SemaphoreType.DMA(s)
     rows = V(128, 768)
     pack_buffer = V(64, 12, 128)
-    recv_o, recv_g, pieces, wrows = pl.pallas_call(
+    out_in, tg_in, pieces, wrows = pl.pallas_call(
         layer_kernel,
-        out_shape=[S(64, 12, 128), S(64, 12, 128), S(8, 12, 384), S(12, 2304)],
+        out_shape=[S(128, 768), S(128, 768), S(8, 12, 384), S(12, 2304)],
         in_specs=[hbm, hbm, vmem, hbm, hbm],
         out_specs=[hbm] * 4,
         scratch_shapes=[rows, V(768, 2304), V(768, 768), V(12, 2304), rows]
@@ -551,10 +568,11 @@
     out, tg, qkv_rows, out_rows, gain_rows = pl.pallas_call(
         finish_kernel,
         out_shape=[S(128, 768), S(128, 768), S(12, 2304), S(12, 768), S(12)],
-        in_specs=[vmem] * 5,
-        out_specs=[vmem] * 5,
+        in_specs=[hbm] * 5,
+        out_specs=[hbm] * 5,
+        scratch_shapes=[rows, rows, V(8, 12, 384), V(12, 2304), V(768), V(12, 2304), V(12, 768), V(12), D(10)],
         compiler_params=pltpu.CompilerParams(vmem_limit_bytes=60 * 2 ** 20),
-    )(recv_o, recv_g, pieces, wrows, norm_gain_vector)
+    )(out_in, tg_in, pieces, wrows, norm_gain_vector)
     return out.reshape(shape), tg.reshape(shape), qkv_rows, out_rows, gain_rows
 
 

time: 84.9 us -> 84.2 us (level)
  Pallas kernels: 84.1 us -> 83.2 us
where the time goes in v5:
time: 84.2 us; the launch traced here: 84 us
  Pallas kernels  83.2 us (99%)
    pallas_call x1, Pallas kernels, body(): pl.pallas_call(layer_kernel, out_shape=[S(128, 768), S(128, 768), S(8, 12...  81 us
    pallas_call x1, Pallas kernels, body(): pl.pallas_call(finish_kernel, out_shape=[S(128, 768), S(128, 768), S(12,...  2.15 us

profile of v5, /device:TPU:1, one launch (start us, length us, event | category | flops | bytes accessed | tf_op | source)
XLA Modules:
  0.0 84.0 jit_solution(7492065158007268124)
XLA Ops:
  0.6 81.0 %shard_map.92 = (f32[128,768]{1,0:T(8,128)}, f32[128,768]{1,0:T(8,128)}, f32[8,12,384]{2,1,0:T(8,128)}, f32[12,2304]{1,0:T(8,128)}) custom-call(f32[128,768]{1,0:T(8,128)} %bitcast.4, f32[128,768]{1,0:T(8,128)} %bitcast.5, f32[768]{0:T(1024)} %gain_hbm.1, f32[768,2304]{1,0:T(8,128)} %wq_hbm.1, f32[768,768]{1,0:T(8,128)} %wo_hbm.1), custom_call_target="tpu_custom_call" | custom-call | tf_op jit(solution)/shard_map/pallas_call | solution.py:553
  81.7 2.2 %shard_map.93 = (f32[128,768]{1,0:T(8,128)}, f32[128,768]{1,0:T(8,128)}, f32[12,2304]{1,0:T(8,128)}, f32[12,768]{1,0:T(8,128)}, f32[12]{0:T(128)}) custom-call(f32[128,768]{1,0:T(8,128)} %get-tuple-element.14.o_hbm, f32[128,768]{1,0:T(8,128)} %get-tuple-element.15.g_hbm, f32[8,12,384]{2,1,0:T(8,128)} %get-tuple-element.16.p_hbm, ...), custom_call_target="tpu_custom_call" | custom-call | tf_op jit(solution)/shard_map/pallas_call | solution.py:568

commit v6 on v5

--- a/solution.py
+++ b/solution.py
@@ -403,7 +403,7 @@
             steps = len(order(k, s))
             if step >= steps:
                 continue
-            reduce_copy(k, s, step, own, terms, landing, sem_red).wait()
+            reduce_copy(k, s, step, own, terms, landing, sem_red).wait_recv()
             reduce_add(k, s, step, own, terms, landing)
             if step < steps - 1:
                 reduce_copy(k, s, step + 1, own, terms, landing, sem_red).start()
@@ -500,6 +500,8 @@
     for copy in copies:
         copy.wait()
     results[3].start()
+    for k, s, step in landings():
+        reduce_copy(k, s, step, own, terms, landing, sem_red).wait_send()
     for result in results:
         result.wait()
 

time: 84.2 us -> 84.1 us (level)
  no operation moved by 1% of the time
where the time goes in v6:
time: 84.1 us; the launch traced here: 84 us
  Pallas kernels  83.2 us (99%)
    pallas_call x1, Pallas kernels, body(): pl.pallas_call(layer_kernel, out_shape=[S(128, 768), S(128, 768), S(8, 12...  81 us
    pallas_call x1, Pallas kernels, body(): pl.pallas_call(finish_kernel, out_shape=[S(128, 768), S(128, 768), S(12,...  2.15 us

profile of v6, /device:TPU:1, one launch (start us, length us, event | category | flops | bytes accessed | tf_op | source)
XLA Modules:
  0.0 84.0 jit_solution(15105372742064064444)
XLA Ops:
  0.6 81.0 %shard_map.92 = (f32[128,768]{1,0:T(8,128)}, f32[128,768]{1,0:T(8,128)}, f32[8,12,384]{2,1,0:T(8,128)}, f32[12,2304]{1,0:T(8,128)}) custom-call(f32[128,768]{1,0:T(8,128)} %bitcast.4, f32[128,768]{1,0:T(8,128)} %bitcast.5, f32[768]{0:T(1024)} %gain_hbm.1, f32[768,2304]{1,0:T(8,128)} %wq_hbm.1, f32[768,768]{1,0:T(8,128)} %wo_hbm.1), custom_call_target="tpu_custom_call" | custom-call | tf_op jit(solution)/shard_map/pallas_call | solution.py:555
  81.7 2.2 %shard_map.93 = (f32[128,768]{1,0:T(8,128)}, f32[128,768]{1,0:T(8,128)}, f32[12,2304]{1,0:T(8,128)}, f32[12,768]{1,0:T(8,128)}, f32[12]{0:T(128)}) custom-call(f32[128,768]{1,0:T(8,128)} %get-tuple-element.14.o_hbm, f32[128,768]{1,0:T(8,128)} %get-tuple-element.15.g_hbm, f32[8,12,384]{2,1,0:T(8,128)} %get-tuple-element.16.p_hbm, ...), custom_call_target="tpu_custom_call" | custom-call | tf_op jit(solution)/shard_map/pallas_call | solution.py:570
